TPU v7x, 256 devices: a whole 4x4x8 slice. The times are simulated.
256 devices in a mesh: dp: 4 (over x_lo, core), ctx: 64 (over y, z, x_hi).
Axes of the slice: x: 4 (x_hi: 2, x_lo: 2; x = x_hi * 2 + x_lo), y: 4, z: 8, core: 2. Of those that a mesh axis runs over, the one named last changes fastest.
Arguments:
- layer_input: bfloat16 [16384, 8192], P('ctx', 'dp'), may hold values from -16 to 16
- conv_output: bfloat16 [16384, 8192], P('ctx', 'dp'), may hold values from -6 to 6
- state_maps: bfloat16 [16384, 256], P('ctx'), may hold values from -0.1875 to 0.1875
- log_decay: float32 [128, 16384], P('dp', 'ctx'), may hold values from -1 to 0, as said below
- out_grad: bfloat16 [16384, 8192], P('ctx', 'dp'), may hold values from -6 to 6
Outputs:
- grad_conv: bfloat16 [16384, 8192], P('ctx', 'dp')
- grad_maps: float32 [16384, 256], P('ctx')
- grad_decay: float32 [128, 16384], P('dp', 'ctx')
- grad_weight: float32 [8192, 256], P(('dp', 'ctx'))
Inputs may be any that keep to these rules, and one draw needn't show every extreme that they name: `log_decay`: negative.
All inputs are finite; a program needn't handle non-finite values.
Results may differ from a plain program's by a relative error of at most 0.0054.
Values sent between devices are 32-bit elements; how exact they have to be, the bound alone decides.
A program may use at most 320 MiB of HBM per device.

v0:
```python
import math

import jax
import jax.numpy as jnp
from jax import lax
from jax.sharding import PartitionSpec as P

BLOCK = 128


def carried_in(part, axis, combine, identity, reverse):
    count = lax.axis_size(axis)
    place = lax.axis_index(axis)
    ahead = count - 1 - place if reverse else place
    gathered = jax.tree.map(lambda a: lax.all_gather(a, axis), part)
    state = jax.tree.map(lambda a, e: jnp.zeros_like(a) + jnp.asarray(e, a.dtype), part, identity)

    def one(lap, state):
        source = count - 1 - lap if reverse else lap
        return combine(
            state, jax.tree.map(lambda a: lax.dynamic_index_in_dim(a, source, 0, False), gathered)
        )

    return lax.fori_loop(0, ahead, one, state)


def block_summary(conv_block, grad_block, maps_block, decay_block):
    head_count = decay_block.shape[0]
    tok_count = conv_block.shape[0]
    head_size = conv_block.shape[1] // head_count
    state_size = maps_block.shape[1] // 2
    cumulative = jnp.cumsum(decay_block, axis=1)
    to_end = jnp.exp(cumulative[:, -1:] - cumulative)
    from_start = jnp.exp(cumulative)
    conv_heads = conv_block.reshape(tok_count, head_count, head_size)
    grad_heads = grad_block.reshape(tok_count, head_count, head_size)
    input_map = maps_block[:, :state_size].astype(jnp.float32)
    output_map = maps_block[:, state_size:].astype(jnp.float32)
    input_weighted = (to_end[:, :, None] * input_map[None]).astype(jnp.bfloat16)
    output_weighted = (from_start[:, :, None] * output_map[None]).astype(jnp.bfloat16)
    final_state = jnp.einsum(
        "thp,htn->hpn", conv_heads, input_weighted, preferred_element_type=jnp.float32
    )
    back_grad = jnp.einsum(
        "thp,htn->hpn", grad_heads, output_weighted, preferred_element_type=jnp.float32
    )
    return (jnp.exp(cumulative[:, -1]), final_state, back_grad)


def block_gradients(
    conv_block, grad_block, maps_block, decay_block, start_state, finish, final_state
):
    head_count = decay_block.shape[0]
    tok_count = conv_block.shape[0]
    head_size = conv_block.shape[1] // head_count
    state_size = maps_block.shape[1] // 2
    group_size = 8
    cumulative = jnp.cumsum(decay_block, axis=1)
    to_end = jnp.exp(cumulative[:, -1:] - cumulative)
    from_start = jnp.exp(cumulative)
    conv_heads = conv_block.reshape(tok_count, head_count, head_size)
    grad_heads = grad_block.reshape(tok_count, head_count, head_size)
    input_low = maps_block[:, :state_size]
    output_low = maps_block[:, state_size:]
    input_map = input_low.astype(jnp.float32)
    output_map = output_low.astype(jnp.float32)
    scores = jnp.dot(output_low, input_low.T, preferred_element_type=jnp.float32)
    positions = jnp.arange(tok_count)
    causal = positions[:, None] >= positions[None, :]

    def one_group(group_index, carried):
        grad_conv, change, mix_total, ingoing_sum, outgoing_sum = carried
        first_head = group_index * group_size

        def heads_of(values, axis_num):
            return lax.dynamic_slice_in_dim(values, first_head, group_size, axis_num)

        conv_group = heads_of(conv_heads, 1)
        grad_group = heads_of(grad_heads, 1)
        cum_group = heads_of(cumulative, 0)
        end_group = heads_of(to_end, 0)
        begin_group = heads_of(from_start, 0)
        start_group = heads_of(start_state, 0)
        finish_group = heads_of(finish, 0)
        final_group = heads_of(final_state, 0)
        spread = cum_group[:, :, None] - cum_group[:, None, :]
        decay_mat = jnp.where(causal[None], jnp.exp(jnp.minimum(spread, 0.0)), 0.0)
        inner_dots = jnp.einsum(
            "thp,shp->hts", grad_group, conv_group, preferred_element_type=jnp.float32
        )
        weight_low = (decay_mat * scores[None]).astype(jnp.bfloat16)
        decay_dots = decay_mat * inner_dots
        mix_total = mix_total + jnp.sum(decay_dots, axis=0)
        start_low = start_group.astype(jnp.bfloat16)
        finish_low = finish_group.astype(jnp.bfloat16)
        finish_b = jnp.einsum(
            "sn,hpn->hsp", input_low, finish_low, preferred_element_type=jnp.float32
        )
        conv_finish = jnp.einsum(
            "thp,hpn->htn", conv_group, finish_low, preferred_element_type=jnp.float32
        )
        grad_start = jnp.einsum(
            "thp,hpn->htn", grad_group, start_low, preferred_element_type=jnp.float32
        )
        conv_delta = jnp.einsum(
            "hut,uhp->thp", weight_low, grad_group, preferred_element_type=jnp.float32
        )
        conv_delta = conv_delta + jnp.transpose(end_group[:, :, None] * finish_b, (1, 0, 2))
        ingoing_sum = ingoing_sum + jnp.sum(end_group[:, :, None] * conv_finish, axis=0)
        outgoing_sum = outgoing_sum + jnp.sum(begin_group[:, :, None] * grad_start, axis=0)
        triple = decay_dots * scores[None]
        end_state = jnp.exp(cum_group[:, -1])[:, None, None] * start_group + final_group
        end_term = jnp.sum(finish_group * end_state, axis=(1, 2))
        change_group = begin_group * jnp.sum(grad_start * output_map[None], axis=2)
        change_group = change_group + jnp.sum(triple, axis=2) - jnp.sum(triple, axis=1)
        change_group = change_group - end_group * jnp.sum(conv_finish * input_map[None], axis=2)
        change_group = change_group.at[:, -1].add(end_term)
        grad_conv = lax.dynamic_update_slice_in_dim(
            grad_conv, conv_delta.astype(jnp.bfloat16), first_head, 1
        )
        change = lax.dynamic_update_slice_in_dim(change, change_group, first_head, 0)
        return (grad_conv, change, mix_total, ingoing_sum, outgoing_sum)

    initial = (
        jnp.zeros((tok_count, head_count, head_size), jnp.bfloat16),
        jnp.zeros((head_count, tok_count), jnp.float32),
        jnp.zeros((tok_count, tok_count), jnp.float32),
        jnp.zeros((tok_count, state_size), jnp.float32),
        jnp.zeros((tok_count, state_size), jnp.float32),
    )
    grad_conv, change, mix_total, ingoing_sum, outgoing_sum = lax.fori_loop(
        0, head_count // group_size, one_group, initial
    )
    grad_decay = jnp.flip(jnp.cumsum(jnp.flip(change, axis=1), axis=1), axis=1)
    return (
        grad_conv.reshape(tok_count, head_count * head_size),
        grad_decay,
        mix_total,
        ingoing_sum,
        outgoing_sum,
    )


def link_states(earlier, latter):
    return (earlier[0] * latter[0], latter[0][:, None, None] * earlier[1] + latter[1])


def apply_mix(mix_stack, ingoing, outgoing, state_maps):
    state_size = state_maps.shape[1] // 2
    highest = lax.Precision.HIGHEST
    parts = []
    for block_num in range(mix_stack.shape[0]):
        lower = block_num * BLOCK
        upper = lower + BLOCK
        input_map = state_maps[lower:upper, :state_size].astype(jnp.float32)
        output_map = state_maps[lower:upper, state_size:].astype(jnp.float32)
        grad_input = (
            jnp.dot(mix_stack[block_num].T, output_map, precision=highest) + ingoing[lower:upper]
        )
        grad_output = (
            jnp.dot(mix_stack[block_num], input_map, precision=highest) + outgoing[lower:upper]
        )
        parts.append(jnp.concatenate([grad_input, grad_output], axis=1))
    return jnp.concatenate(parts, axis=0)


def on_device(layer_input, conv_output, state_maps, log_decay, out_grad):
    tok_count = conv_output.shape[0]
    head_count = log_decay.shape[0]
    block_count = tok_count // BLOCK
    pieces = []
    for block_num in range(block_count):
        lower = block_num * BLOCK
        upper = lower + BLOCK
        pieces.append(
            (
                conv_output[lower:upper],
                out_grad[lower:upper],
                state_maps[lower:upper],
                log_decay[:, lower:upper],
            )
        )
    summaries = []
    for piece_args in pieces:
        summaries.append(block_summary(piece_args[0], piece_args[1], piece_args[2], piece_args[3]))
    unit_decay = jnp.ones((head_count,), jnp.float32)
    zero_state = jnp.zeros_like(summaries[0][1])
    run_decay = unit_decay
    run_state = zero_state
    local_starts = []
    local_before = []
    for block_num in range(block_count):
        local_starts.append(run_state)
        local_before.append(run_decay)
        run_state = summaries[block_num][0][:, None, None] * run_state + summaries[block_num][1]
        run_decay = run_decay * summaries[block_num][0]
    back_decay = unit_decay
    run_grad = zero_state
    local_finishes = [zero_state] * block_count
    local_after = [unit_decay] * block_count
    for block_num in reversed(range(block_count)):
        local_finishes[block_num] = run_grad
        local_after[block_num] = back_decay
        run_grad = summaries[block_num][2] + summaries[block_num][0][:, None, None] * run_grad
        back_decay = back_decay * summaries[block_num][0]
    _, device_start = carried_in(
        (run_decay, run_state), "ctx", link_states, (unit_decay, zero_state), False
    )
    _, device_finish = carried_in(
        (back_decay, run_grad), "ctx", link_states, (unit_decay, zero_state), True
    )
    conv_parts = []
    decay_parts = []
    mix_parts = []
    ingoing_parts = []
    outgoing_parts = []
    for block_num in range(block_count):
        before = local_before[block_num]
        after = local_after[block_num]
        start_state = before[:, None, None] * device_start + local_starts[block_num]
        finish = after[:, None, None] * device_finish + local_finishes[block_num]
        piece_args = pieces[block_num]
        conv_part, decay_part, mix_part, ingoing_part, outgoing_part = block_gradients(
            piece_args[0],
            piece_args[1],
            piece_args[2],
            piece_args[3],
            start_state,
            finish,
            summaries[block_num][1],
        )
        conv_parts.append(conv_part)
        decay_parts.append(decay_part)
        mix_parts.append(mix_part)
        ingoing_parts.append(ingoing_part)
        outgoing_parts.append(outgoing_part)
    grad_conv = jnp.concatenate(conv_parts, axis=0)
    grad_decay = jnp.concatenate(decay_parts, axis=1)
    mix_stack = jnp.stack(mix_parts)
    ingoing = jnp.concatenate(ingoing_parts, axis=0)
    outgoing = jnp.concatenate(outgoing_parts, axis=0)
    mix_all, ingoing_all, outgoing_all = lax.psum((mix_stack, ingoing, outgoing), "dp")
    grad_maps = apply_mix(mix_all, ingoing_all, outgoing_all, state_maps)
    maps_low = grad_maps.astype(jnp.bfloat16)
    grad_scale = 1.0 / math.sqrt(tok_count * lax.axis_size("ctx"))
    contract = (((0,), (0,)), ((), ()))
    grad_weight = lax.psum_scatter(
        lax.dot_general(layer_input, maps_low, contract, preferred_element_type=jnp.float32)
        * grad_scale,
        "ctx",
        scatter_dimension=0,
        tiled=True,
    )
    return (grad_conv, grad_maps, grad_decay, grad_weight)


def solution(mesh):
    placed = (P("ctx", "dp"), P("ctx", "dp"), P("ctx", None), P("dp", "ctx"), P("ctx", "dp"))
    return jax.shard_map(
        on_device,
        mesh=mesh,
        in_specs=placed,
        out_specs=(P("ctx", "dp"), P("ctx", None), P("dp", "ctx"), P(("dp", "ctx"), None)),
        check_vma=False,
    )
```

profile of v0, /device:TPU:2, one launch (start us, length us, event | category | flops | bytes accessed | tf_op | source)
XLA Modules:
  0.0 2003.9 jit_solution(15992650100330657790)
XLA Ops:
  15.7 2.6 fusion.52
  19.9 191.6 %all-reduce = f32[2048]{0:T(1024)S(1)} all-reduce(f32[2048]{0:T(1024)S(1)} %dynamic-update-slice.20), channel_id=2, replica_groups=mesh['dp'=4,'ctx'=64] {'ctx'}, use_global_device_ids=true, to_apply=%add | all-reduce | flops 2048 | bytes 16384
  214.8 1.5 convolution_bitcast_fusion.5
  216.3 419.3 %all-gather.6.cloned.1.call-done = f32[2048,64,128]{2,1,0:T(8,128)} async-done(((f32[32,64,128]{2,1,0:T(8,128)}), f32[2048,64,128]{2,1,0:T(8,128)}) %all-gather.6.cloned.1.call-update) | async-done | bytes 67108880 | tf_op jit(solution)/shard_map/all_gather | solution.py:15
  635.7 94.3 %while.78 = (s32[]{:T(128)}, f32[32,64,128]{2,1,0:T(8,128)S(1)}, s32[]{:T(128)}, f32[64,32]{1,0:T(8,128)S(1)}, f32[64,32,64,128]{3,2,1,0:T(8,128)}, /*index=5*/s32[]{:T(128)}, s32[]{:T(128)}, s32[]{:T(128)}, s32[]{:T(128)}) while((s32[]{:T(128)}, f32[32,64,128]{2,1,0:T(8,128)S(1)}, s32[]{:T(128)}, f32[64,32]{1,0:T(8,128)S(1)}, ...), condition=%wide.region_5.6_spmd, body=%wide.region_4.5_spmd.sunk | while | flops 524294 | bytes 3146259 | solution.py:24
  635.8 1.4 bitcast_add_fusion.4
  637.2 1.4 bitcast_add_fusion.4
  638.7 1.4 bitcast_add_fusion.4
  640.2 1.4 bitcast_add_fusion.4
  641.7 1.4 bitcast_add_fusion.4
  643.2 1.4 bitcast_add_fusion.4
  644.7 1.4 bitcast_add_fusion.4
  646.2 1.4 bitcast_add_fusion.4
  647.7 1.4 bitcast_add_fusion.4
  649.2 1.4 bitcast_add_fusion.4
  650.7 1.4 bitcast_add_fusion.4
  652.2 1.4 bitcast_add_fusion.4
  653.7 1.4 bitcast_add_fusion.4
  655.2 1.4 bitcast_add_fusion.4
  656.7 1.4 bitcast_add_fusion.4
  658.2 1.4 bitcast_add_fusion.4
  659.7 1.4 bitcast_add_fusion.4
  661.2 1.4 bitcast_add_fusion.4
  662.7 1.4 bitcast_add_fusion.4
  664.2 1.4 bitcast_add_fusion.4
  665.7 1.4 bitcast_add_fusion.4
  667.2 1.4 bitcast_add_fusion.4
  668.7 1.4 bitcast_add_fusion.4
  670.2 1.4 bitcast_add_fusion.4
  671.7 1.4 bitcast_add_fusion.4
  674.7 1.4 bitcast_add_fusion.4
  689.6 1.4 bitcast_add_fusion.4
  703.1 1.4 bitcast_add_fusion.4
  718.1 1.4 bitcast_add_fusion.4
  730.1 3.9 multiply_add_fusion.2
  737.3 1.5 fusion.68
  738.8 1.6 fusion.63
  740.4 593.9 %all-gather.8.cloned.1.call-done = f32[2048,64,128]{2,1,0:T(8,128)} async-done(((f32[32,64,128]{2,1,0:T(8,128)}), f32[2048,64,128]{2,1,0:T(8,128)}) %all-gather.8.cloned.1.call-update) | async-done | bytes 67108880 | tf_op jit(solution)/shard_map/all_gather | solution.py:15
  1334.4 2.4 multiply_add_fusion
  1338.3 68.4 %while.80 = (s32[]{:T(128)}, bf16[128,32,64]{0,2,1:T(8,128)(2,1)}, f32[32,128]{1,0:T(8,128)}, f32[128,128]{1,0:T(8,128)S(1)}, f32[128,128]{0,1:T(8,128)S(1)}, /*...) while((s32[]{:T(128)}, bf16[128,32,64]{0,2,1:T(8,128)(2,1)}, ...), condition=%wide.region_16.17_spmd.clone, body=%wide.region_7.16_spmd.clone.sunk | while | flops 87163912 | bytes 4264715 | solution.py:131
  1340.9 1.9 fusion.99
  1342.8 2.1 multiply_reduce_fusion.24
  1345.6 1.9 multiply_reduce_fusion.23
  1348.2 1.8 multiply_reduce_fusion.25
  1358.0 1.9 fusion.99
  1359.9 2.1 multiply_reduce_fusion.24
  1362.7 1.9 multiply_reduce_fusion.23
  1365.3 1.8 multiply_reduce_fusion.25
  1375.1 1.9 fusion.99
  1377.0 2.1 multiply_reduce_fusion.24
  1379.8 1.9 multiply_reduce_fusion.23
  1382.4 1.8 multiply_reduce_fusion.25
  1392.2 1.9 fusion.99
  1394.1 2.1 multiply_reduce_fusion.24
  1396.9 1.9 multiply_reduce_fusion.23
  1399.5 1.8 multiply_reduce_fusion.25
  1406.9 40.9 %while.81 = (s32[]{:T(128)}, bf16[128,32,64]{0,2,1:T(8,128)(2,1)S(1)}, f32[32,128]{1,0:T(8,128)S(1)}, f32[128,128]{1,0:T(8,128)S(1)}, f32[128,128]{0,1:T(8,128)S...) while((s32[]{:T(128)}, ...), condition=%wide.region_26.27_spmd.clone, body=%wide.region_17.26_spmd.clone.sunk | while | flops 87163912 | bytes 4395843 | solution.py:131
  1410.6 1.5 multiply_reduce_fusion.28
  1420.8 1.5 multiply_reduce_fusion.28
  1431.1 1.5 multiply_reduce_fusion.28
  1441.3 1.5 multiply_reduce_fusion.28
  1449.9 173.8 %all-reduce.4.cloned.1.call-done = (f32[256,128]{0,1:T(8,128)}, f32[2,128,128]{2,1,0:T(8,128)}, f32[256,128]{0,1:T(8,128)}) async-done(((f32[256,128]{0,1:T(8,128)}, f32[2,128,128]{2,1,0:T(8,128)}, f32[256,128]{0,1:T(8,128)}), (f32[256,128]{0,1:T(8,128)}, f32[2,128,128]{2,1,0:T(8,128)}, f32[256,128]{0,1:T(8,128)})) %all-reduce.4.cloned.1.call-update) | async-done | bytes 393232 | tf_op jit(solution)/shard_map/psum | solution.py:242
  1628.5 1.9 copy.107
  1635.0 362.3 %reduce-scatter.4.cloned.1.call-done = f32[32,256]{1,0:T(8,128)} async-done(((f32[2048,256]{1,0:T(8,128)}), f32[32,256]{1,0:T(8,128)}) %reduce-scatter.4.cloned.1.call-update) | async-done | bytes 32784
  (392 shorter events, 150.4 us)
Async XLA Ops:
  7.2 1620.9 %copy-start = (bf16[256,2048]{1,0:T(8,128)(2,1)S(1)}, bf16[256,2048]{1,0:T(8,128)(2,1)}, u32[]{:S(2)}) copy-start(bf16[256,2048]{1,0:T(8,128)(2,1)} %param.17) | copy-start | bytes 3145732
  7.2 628.4 %all-gather.6.cloned.1.call-start = ((), (), s32[]{:S(2)}) async-start(), calls=%async_computation.1 | async-start | bytes 68157440 | tf_op jit(solution)/shard_map/all_gather | solution.py:15
  9.2 2.4 copy-start.16
  11.6 3.2 copy-start.14
  11.6 718.5 %copy-start.12 = (f32[32,128]{1,0:T(8,128)}, f32[32,128]{1,0:T(8,128)S(1)}, u32[]{:S(2)}) copy-start(f32[32,128]{1,0:T(8,128)S(1)} %get-tuple-element.1993) | copy-start | bytes 49156
  12.4 199.2 %copy-start.10 = (bf16[128,128]{1,0:T(8,128)(2,1)}, bf16[128,128]{1,0:T(8,128)(2,1)S(1)}, u32[]{:S(2)}) copy-start(bf16[128,128]{1,0:T(8,128)(2,1)S(1)} %get-tuple-element.2067) | copy-start | bytes 98308
  12.4 201.1 %copy-start.9 = (bf16[128,128]{1,0:T(8,128)(2,1)}, bf16[128,128]{1,0:T(8,128)(2,1)S(1)}, u32[]{:S(2)}) copy-start(bf16[128,128]{1,0:T(8,128)(2,1)S(1)} %get-tuple-element.1995) | copy-start | bytes 98308
  14.3 4.0 copy-start.4
  14.8 3.5 copy-start.5
  15.6 197.6 %copy-start.2 = (f32[32,64,128]{2,1,0:T(8,128)}, f32[32,64,128]{2,1,0:T(8,128)S(1)}, u32[]{:S(2)}) copy-start(f32[32,64,128]{2,1,0:T(8,128)S(1)} %fusion.51) | copy-start | bytes 3145732
  15.6 2.8 copy-start.23
  18.3 1315.9 %all-gather.8.cloned.1.call-start = ((), (), s32[]{:S(2)}) async-start(), calls=%async_computation.2 | async-start | bytes 68157440 | tf_op jit(solution)/shard_map/all_gather | solution.py:15
  213.5 422.1 %copy-start.3 = (bf16[128,2048]{0,1:T(8,128)(2,1)}, bf16[128,2048]{0,1:T(8,128)(2,1)S(1)}, u32[]{:S(2)}) copy-start(bf16[128,2048]{0,1:T(8,128)(2,1)S(1)} %copy.98) | copy-start | bytes 1572868
  216.3 513.7 %copy-start.1 = (f32[32,64,128]{2,1,0:T(8,128)}, f32[32,64,128]{2,1,0:T(8,128)S(1)}, u32[]{:S(2)}) copy-start(f32[32,64,128]{2,1,0:T(8,128)S(1)} %convolution_bitcast_fusion.5) | copy-start | bytes 3145732
  730.0 4.0 copy-start.22
  734.0 889.6 %all-reduce.4.cloned.1.call-start = ((), (), s32[]{:S(2)}) async-start(), calls=%async_computation.4 | async-start | bytes 786432 | tf_op jit(solution)/shard_map/psum | solution.py:242
  1338.3 7.3 copy-start.19
  1338.3 9.9 copy-start.20
  1355.4 7.3 copy-start.19
  1355.4 9.9 copy-start.20
  1372.5 7.3 copy-start.19
  1372.5 9.9 copy-start.20
  1389.6 7.3 copy-start.19
  1389.6 9.9 copy-start.20
  1406.8 216.8 %copy-start.11 = (bf16[256,256]{1,0:T(8,128)(2,1)S(1)}, bf16[256,256]{1,0:T(8,128)(2,1)}, u32[]{:S(2)}) copy-start(bf16[256,256]{1,0:T(8,128)(2,1)} %param.19) | copy-start | bytes 393220
  1406.9 5.2 copy-start.13
  1406.9 5.2 copy-start.17
  1406.9 6.5 copy-start.15
  1406.9 6.5 copy-start.18
  1417.1 5.2 copy-start.13
  1417.1 5.2 copy-start.17
  1417.1 6.4 copy-start.15
  1417.2 6.4 copy-start.18
  1427.3 5.2 copy-start.13
  1427.3 5.2 copy-start.17
  1427.3 6.4 copy-start.15
  1427.4 6.4 copy-start.18
  1437.5 5.2 copy-start.13
  1437.6 5.2 copy-start.17
  1437.6 6.4 copy-start.15
  1437.6 6.4 copy-start.18
  1447.7 179.2 %copy-start.6 = (bf16[128,32,64]{0,2,1:T(8,128)(2,1)}, bf16[128,32,64]{0,2,1:T(8,128)(2,1)S(1)}, u32[]{:S(2)}) copy-start(bf16[128,32,64]{0,2,1:T(8,128)(2,1)S(1)} %get-tuple-element.1199) | copy-start | bytes 1572868
  1449.8 547.5 %reduce-scatter.4.cloned.1.call-start = ((), (), s32[]{:S(2)}) async-start(), calls=%async_computation.3 | async-start | bytes 2129920
  1630.4 0.7 copy-start.21
  1630.4 1.6 copy-start.7
  1630.4 1.6 copy-start.8
Sparse Core Ops, SparseCore 0:
  18.5 617.0 all-gather.5
  734.1 600.0 all-gather.7
  1449.9 173.6 all-reduce.3
  1630.6 366.7 reduce-scatter.3
where the time goes:
time: 2010 us; the launch traced here: 2000 us
  waiting for transfers between devices  1550 us (77%)
  blocking collectives  192 us (10%)
  other arithmetic  130 us (6%)
  matrix products  77.5 us (4%)
  local copies, waits for them, and re-layouts  37.6 us (2%)
    all_gather x2, waiting for transfers between devices, carried_in(): gathered = jax.tree.map(lambda a: lax.all_gather(a, axis), part)  1010 us
    unnamed x5, waiting for transfers between devices  362 us
    unnamed x1, blocking collectives  192 us
    psum x1, waiting for transfers between devices, on_device(): lax.psum((mix_stack, ingoing, outgoing), 'dp')  174 us
    add x63, other arithmetic, link_states(): latter[0][:, None, None] * earlier[1] + latter[1]  91.2 us
  transfers between devices with their start and end apart: 4, of which 4 were waited for; matrix products, arithmetic and copies ran while one was open for 1% of the time, Pallas kernels for 0%

commit v1 on v0

v1 whole, which is shorter than its diff:
```python
import functools
import math

import jax
import jax.numpy as jnp
from jax import lax
from jax.experimental import pallas as pl
from jax.experimental.pallas import tpu as pltpu
from jax.sharding import PartitionSpec as P

BLOCK = 128
HEAD = 64
STATE = 128
PAIR = 2 * HEAD
ROWS = PAIR + 8
Z_SIZE = 8
Y_SIZE = 4
FAR_FIRST = (4, 3, 5, 2, 6, 1, 7)
MESH = pl.DeviceIdType.MESH
F32 = jnp.float32
BF16 = jnp.bfloat16
HIGHEST = lax.Precision.HIGHEST
NT = (((1,), (1,)), ((), ()))
TN = (((0,), (0,)), ((), ()))
NN = (((1,), (0,)), ((), ()))
VMEM = pl.BlockSpec(memory_space=pltpu.VMEM)
LIMIT = 56 * 1024 * 1024


def dot(a, b, dims=NN, precision=None):
    return lax.dot_general(a, b, dims, precision=precision, preferred_element_type=F32)


def iota(shape, axis):
    return lax.broadcasted_iota(jnp.int32, shape, axis)


def two_parts(values):
    high = values.astype(BF16)
    return high, (values - high.astype(F32)).astype(BF16)


def head_lanes(first_head, head_count, columns, width):
    shape = (head_count, columns)
    return (iota(shape, 0) == first_head + iota(shape, 1) // width).astype(BF16)


def widen(parts, lanes):
    return dot(parts[0], lanes) + dot(parts[1], lanes)


def summary_kernel(conv, grad, maps, decay, ahead, behind):
    heads, toks = decay.shape
    group = 8 * HEAD
    decays = decay[...]
    lower = (iota((toks, toks), 1) <= iota((toks, toks), 0)).astype(F32)
    cum = dot(lower, decays, NT, HIGHEST)
    to_end = two_parts(jnp.exp(cum[toks - 1 : toks, :] - cum))
    from_start = two_parts(jnp.exp(cum))
    total = jnp.exp(dot(decays, jnp.ones((toks, STATE), F32), NN, HIGHEST))
    spread = (iota((heads * 4, heads), 0) // 4 == iota((heads * 4, heads), 1)).astype(F32)
    tiles = dot(spread, total, NN, HIGHEST).reshape(heads // 2, 8, STATE)
    ahead[:, PAIR:, :] = tiles
    behind[:, PAIR:, :] = tiles
    input_map = maps[:, :STATE]
    output_map = maps[:, STATE:]
    for part in range(heads * HEAD // group):
        columns = slice(part * group, (part + 1) * group)
        slices = slice(part * group // PAIR, (part + 1) * group // PAIR)
        lanes = head_lanes(part * group // HEAD, heads, group, HEAD)
        weighted = (widen(to_end, lanes) * conv[:, columns].astype(F32)).astype(BF16)
        ahead[slices, :PAIR, :] = dot(weighted, input_map, TN).reshape(-1, PAIR, STATE)
        weighted = (widen(from_start, lanes) * grad[:, columns].astype(F32)).astype(BF16)
        behind[slices, :PAIR, :] = dot(weighted, output_map, TN).reshape(-1, PAIR, STATE)


def place():
    dp, ctx = lax.axis_index("dp"), lax.axis_index("ctx")
    return dp, ctx // (2 * Z_SIZE), (ctx // 2) % Z_SIZE, ctx % 2


def device(dp, y, z, x):
    return (dp, (y * Z_SIZE + z) * 2 + x)


def greet(partners):
    barrier = pltpu.get_barrier_semaphore()
    for partner in partners:
        pl.semaphore_signal(barrier, inc=1, device_id=partner, device_id_type=MESH)
    pl.semaphore_wait(barrier, len(partners))


def remote(src, dst, send, recv, target):
    return pltpu.make_async_remote_copy(
        src_ref=src, dst_ref=dst, send_sem=send, recv_sem=recv, device_id=target, device_id_type=MESH
    )


def per_head(tile, values):
    return jnp.concatenate([values[:HEAD] * tile[0:1], values[HEAD:] * tile[4:5]], axis=0)


def carry_kernel(
    ahead, behind, start, finish,
    x_in, t_out, z_in, y_in, before, back_out, back_in, x_out,
    x_send, x_recv, z_send, z_recv, y_send, y_recv, b_send, b_recv, r_send, r_recv,
):
    dp, y, z, x = place()
    other = device(dp, y, z, 1 - x)
    z_at = [device(dp, y, (z + k) % Z_SIZE, x) for k in range(Z_SIZE)]
    y_at = [device(dp, (y + m) % Y_SIZE, z, x) for m in range(Y_SIZE)]
    greet([other] + z_at[1:] + y_at[1:])
    own = (ahead, behind)
    result = (start, finish)
    order = FAR_FIRST + (0,)
    sent = []

    def x_copy(way, k):
        piece = (z + k) % Z_SIZE
        return remote(
            own[way].at[(1 - x) * Z_SIZE + piece], x_in.at[way, piece],
            x_send.at[way, k], x_recv.at[way, k], other,
        )

    def z_copy(way, k):
        return remote(t_out.at[way, k], z_in.at[way, k], z_send.at[way, k], z_recv.at[way, k], z_at[k])

    def y_copy(way, m):
        return remote(y_in.at[way, 0], y_in.at[way, m], y_send.at[way, m], y_recv.at[way, m], y_at[m])

    def b_copy(way, k):
        return remote(
            back_out.at[way, k], back_in.at[way, k], b_send.at[way, k], b_recv.at[way, k], z_at[k]
        )

    def r_copy(way, k):
        piece = x * Z_SIZE + (z + Z_SIZE - k) % Z_SIZE
        return remote(
            x_out.at[way, k], result[way].at[piece], r_send.at[way, k], r_recv.at[way, k], other
        )

    def begin(copy):
        copy.start()
        sent.append(copy)

    for way in range(2):
        for k in order:
            begin(x_copy(way, k))

    def join(way):
        first = x == way
        for k in order:
            x_copy(way, k).wait_recv()
            piece = (z + k) % Z_SIZE
            mine = own[way][x * Z_SIZE + piece]
            theirs = x_in[way, piece]
            early = jnp.where(first, mine, theirs)
            late = jnp.where(first, theirs, mine)
            state = per_head(late[PAIR:], early[:PAIR]) + late[:PAIR]
            target = z_in.at[way, 0] if k == 0 else t_out.at[way, k]
            target[:PAIR] = state
            target[PAIR:] = early[PAIR:] * late[PAIR:]
            if k:
                begin(z_copy(way, k))

    def scan(way):
        for k in FAR_FIRST:
            z_copy(way, k).wait_recv()
        state = jnp.zeros((PAIR, STATE), F32)
        decay = jnp.ones((8, STATE), F32)
        for step in range(Z_SIZE):
            at = Z_SIZE - 1 - step if way else step
            slot = (z + Z_SIZE - at) % Z_SIZE
            out = (at + Z_SIZE - z) % Z_SIZE
            before[way, out, :PAIR] = state
            before[way, out, PAIR:] = decay
            tile = z_in[way, slot, PAIR:]
            state = per_head(tile, state) + z_in[way, slot, :PAIR]
            decay = decay * tile
        y_in[way, 0, :PAIR] = state
        y_in[way, 0, PAIR:] = decay
        for m in range(1, Y_SIZE):
            begin(y_copy(way, m))

    def spread(way):
        for m in range(1, Y_SIZE):
            y_copy(way, m).wait_recv()
        state = jnp.zeros((PAIR, STATE), F32)
        for step in range(Y_SIZE):
            at = Y_SIZE - 1 - step if way else step
            slot = (y + Y_SIZE - at) % Y_SIZE
            counts = (at > y) if way else (at < y)
            new = per_head(y_in[way, slot, PAIR:], state) + y_in[way, slot, :PAIR]
            state = jnp.where(counts, new, state)
        for k in order:
            target = back_in.at[way, 0] if k == 0 else back_out.at[way, k]
            target[...] = before[way, k, :PAIR] + per_head(before[way, k, PAIR:], state)
            if k:
                begin(b_copy(way, k))

    def hand_on(way):
        first = x == way
        for k in (0, 1, 7, 2, 6, 3, 5, 4):
            if k:
                b_copy(way, k).wait_recv()
            piece = (z + Z_SIZE - k) % Z_SIZE
            early = back_in[way, k]
            left = jnp.where(first, own[way][x * Z_SIZE + piece], x_in[way, piece])
            late = per_head(left[PAIR:], early) + left[:PAIR]
            x_out[way, k] = jnp.where(first, late, early)
            result[way][x * Z_SIZE + piece] = jnp.where(first, early, late)
            begin(r_copy(way, k))

    join(0)
    join(1)
    scan(0)
    scan(1)
    spread(0)
    spread(1)
    hand_on(0)
    hand_on(1)
    for way in range(2):
        for k in order:
            r_copy(way, k).wait_recv()
    for copy in sent:
        copy.wait_send()


def block_kernel(
    conv, grad, maps, decay, start, finish, grad_conv, grad_decay, grad_maps,
    cum_rows, total_rows, change, ends, mix, ingoing, outgoing,
):
    heads, toks = decay.shape
    count = toks // BLOCK
    width = 4 * HEAD
    square = (BLOCK, BLOCK)
    causal = iota(square, 1) <= iota(square, 0)
    lower = causal.astype(F32)
    cum_parts, to_end, from_start, scores = [], [], [], []
    for block in range(count):
        rows = slice(block * BLOCK, (block + 1) * BLOCK)
        decays = decay[:, rows]
        cum = dot(lower, decays, NT, HIGHEST)
        high, middle = two_parts(cum)
        low = (cum - high.astype(F32) - middle.astype(F32)).astype(BF16)
        cum_parts.append((high, middle, low))
        to_end.append(two_parts(jnp.exp(cum[BLOCK - 1 : BLOCK, :] - cum)))
        from_start.append(two_parts(jnp.exp(cum)))
        cum_rows[block] = jnp.broadcast_to(dot(decays, lower, NT, HIGHEST)[:, None, :], (heads, 8, BLOCK))
        total = jnp.exp(dot(decays, jnp.ones((BLOCK, STATE), F32), NN, HIGHEST))
        total_rows[block] = jnp.broadcast_to(total[:, None, :], (heads, 8, STATE))
        scores.append(dot(maps[rows, STATE:], maps[rows, :STATE], NT))
    change[...] = jnp.zeros_like(change)
    mix[...] = jnp.zeros_like(mix)
    ingoing[...] = jnp.zeros_like(ingoing)
    outgoing[...] = jnp.zeros_like(outgoing)

    def one_group(index, _):
        columns = pl.ds(pl.multiple_of(index * width, width), width)
        group_heads = pl.ds(index * 4, 4)
        lanes = head_lanes(index * 4, heads, width, HEAD)
        broad = head_lanes(index * 4, heads, 4 * BLOCK, BLOCK)
        in_first = iota((BLOCK, PAIR), 1) < HEAD

        def decayed(block, state):
            return (state.reshape(4, 8, 8, STATE) * total_rows[block, group_heads][:, None]).reshape(width, STATE)

        x, g, te, fs, xw, gw, final, back = [], [], [], [], [], [], [], []
        for block in range(count):
            rows = slice(block * BLOCK, (block + 1) * BLOCK)
            x.append(conv[rows, columns])
            g.append(grad[rows, columns])
            te.append(widen(to_end[block], lanes))
            fs.append(widen(from_start[block], lanes))
            xw.append((te[block] * x[block].astype(F32)).astype(BF16))
            gw.append((fs[block] * g[block].astype(F32)).astype(BF16))
            final.append(dot(xw[block], maps[rows, :STATE], TN))
            back.append(dot(gw[block], maps[rows, STATE:], TN))
        starts = [start[pl.ds(index * 2, 2)].reshape(width, STATE)]
        for block in range(count):
            starts.append(decayed(block, starts[block]) + final[block])
        finishes = [finish[pl.ds(index * 2, 2)].reshape(width, STATE)]
        for block in reversed(range(1, count)):
            finishes.insert(0, decayed(block, finishes[0]) + back[block])
        for block in range(count):
            rows = slice(block * BLOCK, (block + 1) * BLOCK)
            input_map, output_map = maps[rows, :STATE], maps[rows, STATE:]
            ends[block, group_heads] = jnp.sum(
                (finishes[block] * starts[block + 1]).reshape(4, 8, 8, STATE), axis=1
            )
            start_low = starts[block].astype(BF16)
            finish_low = finishes[block].astype(BF16)
            ingoing[block] += dot(xw[block], finish_low)
            outgoing[block] += dot(gw[block], start_low)
            from_finish = te[block] * dot(input_map, finish_low, NT)
            from_state = fs[block] * dot(output_map, start_low, NT)
            column = sum(dot(part, broad) for part in cum_parts[block])
            y_parts, d_parts, mixed = [], [], None
            for pair in range(2):
                lane = slice(pair * PAIR, (pair + 1) * PAIR)
                x_pair, g_pair = x[block][:, lane], g[block][:, lane]
                zero = jnp.zeros_like(x_pair)
                x_own = [jnp.where(in_first, x_pair, zero), jnp.where(in_first, zero, x_pair)]
                g_own = [jnp.where(in_first, g_pair, zero), jnp.where(in_first, zero, g_pair)]
                weights = []
                for one in range(2):
                    head = 2 * pair + one
                    col = column[:, head * BLOCK : (head + 1) * BLOCK].reshape(16, 8, BLOCK)
                    gap = (col - cum_rows[block, index * 4 + head][None]).reshape(square)
                    falls = jnp.exp(jnp.where(causal, gap, -1e30))
                    inner = dot(g_own[one], x_pair, NT)
                    weights.append((falls * scores[block]).astype(BF16))
                    term = falls * inner
                    mixed = term if mixed is None else mixed + term
                y_parts.append(
                    dot(jnp.concatenate(weights, axis=1), jnp.concatenate(x_own, axis=0))
                )
                d_parts.append(
                    dot(jnp.concatenate(weights, axis=0), jnp.concatenate(g_own, axis=0), TN)
                )
            mix[block] += mixed
            y_all = jnp.concatenate(y_parts, axis=1) + from_state
            d_all = jnp.concatenate(d_parts, axis=1) + from_finish
            grad_conv[rows, columns] = d_all.astype(BF16)
            product = g[block].astype(F32) * y_all - x[block].astype(F32) * d_all
            high, low = two_parts(product)
            change[block] += dot(lanes, high, NT) + dot(lanes, low, NT)
        return 0

    lax.fori_loop(0, heads * HEAD // width, one_group, 0)
    for block in range(count):
        rows = slice(block * BLOCK, (block + 1) * BLOCK)
        input_map, output_map = maps[rows, :STATE].astype(F32), maps[rows, STATE:].astype(F32)
        grad_maps[rows, :STATE] = dot(mix[block], output_map, TN, HIGHEST) + ingoing[block]
        grad_maps[rows, STATE:] = dot(mix[block], input_map, NN, HIGHEST) + outgoing[block]
        end_term = jnp.sum(jnp.sum(ends[block], axis=1), axis=1, keepdims=True)
        at_last = iota((heads, BLOCK), 1) == BLOCK - 1
        changes = change[block] + jnp.where(at_last, end_term, 0.0)
        grad_decay[:, rows] = dot(changes, lower, NN, HIGHEST)


def weight_kernel(
    scale, part, layer, total, weight,
    gathered, flipped, by_z, by_y, z_in, y_in, z_sum, y_sum, z_late, y_late, x_own, x_in,
    p_send, p_recv, g_send, g_recv, z_send, z_recv, y_send, y_recv,
    zl_send, zl_recv, yl_send, yl_recv, x_send, x_recv,
):
    dp, y, z, x = place()
    other = device(dp, y, z, 1 - x)
    z_at = [device(dp, y, (z + k) % Z_SIZE, x) for k in range(Z_SIZE)]
    y_at = [device(dp, (y + m) % Y_SIZE, z, x) for m in range(Y_SIZE)]
    p_at = [device((dp + m) % 4, y, z, x) for m in range(4)]
    greet([other] + z_at[1:] + y_at[1:] + p_at[1:])
    toks = part.shape[0]
    share = toks // 4
    sent = []

    def begin(copy):
        copy.start()
        sent.append(copy)

    def p_copy(m):
        rows = pl.ds(pl.multiple_of((dp + m) % 4 * share, share), share)
        return remote(part.at[rows], gathered.at[m], p_send.at[m], p_recv.at[m], p_at[m])

    def g_copy(m):
        rows = pl.ds(pl.multiple_of(dp * share, share), share)
        return remote(total.at[rows], total.at[rows], g_send.at[m], g_recv.at[m], p_at[m])

    def z_copy(k):
        return remote(by_z.at[(z + k) % Z_SIZE], z_in.at[k], z_send.at[k], z_recv.at[k], z_at[k])

    def y_copy(m):
        return remote(by_y.at[(y + m) % Y_SIZE], y_in.at[m], y_send.at[m], y_recv.at[m], y_at[m])

    def y_late_copy(m):
        return remote(
            z_sum.at[(y + m) % Y_SIZE], y_late.at[m], yl_send.at[m], yl_recv.at[m], y_at[m]
        )

    def z_late_copy(k):
        return remote(
            y_sum.at[(z + k) % Z_SIZE], z_late.at[k], zl_send.at[k], zl_recv.at[k], z_at[k]
        )

    def x_copy(half):
        return remote(
            x_own.at[half, 1 - x], x_in.at[half], x_send.at[half], x_recv.at[half], other
        )

    for m in range(1, 4):
        begin(p_copy(m))
    span = layer.shape[1] // Y_SIZE
    for piece in range(Y_SIZE):
        flipped[piece] = layer[:, piece * span : (piece + 1) * span].T
    mine = pl.ds(pl.multiple_of(dp * share, share), share)
    for m in range(1, 4):
        p_copy(m).wait_recv()
    total[mine] = part[mine] + gathered[1] + gathered[2] + gathered[3]
    for m in range(1, 4):
        begin(g_copy(m))
    for m in range(1, 4):
        g_copy(m).wait_recv()
    low = total[...].astype(BF16)
    for piece in range(Y_SIZE):
        made = dot(flipped[piece], low) * scale
        made = made.reshape(Z_SIZE, span // Z_SIZE, 2 * STATE)
        by_z[:, piece] = made[:, :, :STATE]
        by_y[piece] = made[:, :, STATE:]
    for k in FAR_FIRST[:3]:
        begin(z_copy(k))
    for m in (2, 1, 3):
        begin(y_copy(m))
    for k in FAR_FIRST[3:]:
        begin(z_copy(k))
    for m in range(1, Y_SIZE):
        y_copy(m).wait_recv()
    y_sum[...] = by_y[y] + y_in[1] + y_in[2] + y_in[3]
    for k in FAR_FIRST:
        begin(z_late_copy(k))
    for k in range(1, Z_SIZE):
        z_copy(k).wait_recv()
    z_sum[...] = by_z[z] + sum(z_in[k] for k in range(1, Z_SIZE))
    for m in (2, 1, 3):
        begin(y_late_copy(m))
    for k in range(1, Z_SIZE):
        z_late_copy(k).wait_recv()
    x_own[1] = (y_sum[z] + sum(z_late[k] for k in range(1, Z_SIZE))).reshape(2, -1, STATE)
    begin(x_copy(1))
    for m in range(1, Y_SIZE):
        y_late_copy(m).wait_recv()
    x_own[0] = (z_sum[y] + sum(y_late[m] for m in range(1, Y_SIZE))).reshape(2, -1, STATE)
    begin(x_copy(0))
    for half in (1, 0):
        x_copy(half).wait_recv()
        weight[:, half * STATE : (half + 1) * STATE] = x_own[half, x] + x_in[half]
    for copy in sent:
        copy.wait_send()


def dma(*shape):
    return pltpu.SemaphoreType.DMA(shape)


def on_device(layer_input, conv_output, state_maps, log_decay, out_grad):
    toks, columns = conv_output.shape
    heads = log_decay.shape[0]
    slices = heads // 2
    half = slices // 2
    packed = jax.ShapeDtypeStruct((slices, ROWS, STATE), F32)
    plain = jax.ShapeDtypeStruct((slices, PAIR, STATE), F32)
    ahead, behind = pl.pallas_call(
        summary_kernel,
        out_shape=(packed, packed),
        in_specs=[VMEM] * 4,
        out_specs=(VMEM, VMEM),
        compiler_params=pltpu.CompilerParams(vmem_limit_bytes=LIMIT),
        name="summary",
    )(conv_output, out_grad, state_maps, log_decay)
    start, finish = pl.pallas_call(
        carry_kernel,
        out_shape=(plain, plain),
        in_specs=[VMEM] * 2,
        out_specs=(VMEM, VMEM),
        scratch_shapes=[
            pltpu.VMEM((2, half, ROWS, STATE), F32),
            pltpu.VMEM((2, Z_SIZE, ROWS, STATE), F32),
            pltpu.VMEM((2, Z_SIZE, ROWS, STATE), F32),
            pltpu.VMEM((2, Y_SIZE, ROWS, STATE), F32),
            pltpu.VMEM((2, Z_SIZE, ROWS, STATE), F32),
            pltpu.VMEM((2, Z_SIZE, PAIR, STATE), F32),
            pltpu.VMEM((2, Z_SIZE, PAIR, STATE), F32),
            pltpu.VMEM((2, Z_SIZE, PAIR, STATE), F32),
            dma(2, Z_SIZE), dma(2, Z_SIZE), dma(2, Z_SIZE), dma(2, Z_SIZE),
            dma(2, Y_SIZE), dma(2, Y_SIZE), dma(2, Z_SIZE), dma(2, Z_SIZE),
            dma(2, Z_SIZE), dma(2, Z_SIZE),
        ],
        compiler_params=pltpu.CompilerParams(
            collective_id=0, has_side_effects=True, vmem_limit_bytes=LIMIT
        ),
        name="carry",
    )(ahead, behind)
    count = toks // BLOCK
    grad_conv, grad_decay, part = pl.pallas_call(
        block_kernel,
        out_shape=(
            jax.ShapeDtypeStruct((toks, columns), BF16),
            jax.ShapeDtypeStruct((heads, toks), F32),
            jax.ShapeDtypeStruct((toks, 2 * STATE), F32),
        ),
        in_specs=[VMEM] * 6,
        out_specs=(VMEM,) * 3,
        scratch_shapes=[
            pltpu.VMEM((count, heads, 8, BLOCK), F32),
            pltpu.VMEM((count, heads, 8, STATE), F32),
            pltpu.VMEM((count, heads, BLOCK), F32),
            pltpu.VMEM((count, heads, 8, STATE), F32),
            pltpu.VMEM((count, BLOCK, BLOCK), F32),
            pltpu.VMEM((count, BLOCK, STATE), F32),
            pltpu.VMEM((count, BLOCK, STATE), F32),
        ],
        compiler_params=pltpu.CompilerParams(vmem_limit_bytes=LIMIT),
        name="blocks",
    )(conv_output, out_grad, state_maps, log_decay, start, finish)
    span = columns // Y_SIZE
    tile = span // Z_SIZE
    grad_maps, grad_weight = pl.pallas_call(
        functools.partial(weight_kernel, 1.0 / math.sqrt(toks * lax.axis_size("ctx"))),
        out_shape=(
            jax.ShapeDtypeStruct((toks, 2 * STATE), F32),
            jax.ShapeDtypeStruct((tile // 2, 2 * STATE), F32),
        ),
        in_specs=[VMEM] * 2,
        out_specs=(VMEM, VMEM),
        scratch_shapes=[
            pltpu.VMEM((4, toks // 4, 2 * STATE), F32),
            pltpu.VMEM((Y_SIZE, span, toks), BF16),
            pltpu.VMEM((Z_SIZE, Y_SIZE, tile, STATE), F32),
            pltpu.VMEM((Y_SIZE, Z_SIZE, tile, STATE), F32),
            pltpu.VMEM((Z_SIZE, Y_SIZE, tile, STATE), F32),
            pltpu.VMEM((Y_SIZE, Z_SIZE, tile, STATE), F32),
            pltpu.VMEM((Y_SIZE, tile, STATE), F32),
            pltpu.VMEM((Z_SIZE, tile, STATE), F32),
            pltpu.VMEM((Z_SIZE, tile, STATE), F32),
            pltpu.VMEM((Y_SIZE, tile, STATE), F32),
            pltpu.VMEM((2, 2, tile // 2, STATE), F32),
            pltpu.VMEM((2, tile // 2, STATE), F32),
            dma(4), dma(4), dma(4), dma(4),
            dma(Z_SIZE), dma(Z_SIZE), dma(Y_SIZE), dma(Y_SIZE),
            dma(Z_SIZE), dma(Z_SIZE), dma(Y_SIZE), dma(Y_SIZE),
            dma(2), dma(2),
        ],
        compiler_params=pltpu.CompilerParams(
            collective_id=1, has_side_effects=True, vmem_limit_bytes=LIMIT
        ),
        name="weight",
    )(part, layer_input)
    return (grad_conv, grad_maps, grad_decay, grad_weight)


def solution(mesh):
    placed = (P("ctx", "dp"), P("ctx", "dp"), P("ctx", None), P("dp", "ctx"), P("ctx", "dp"))
    return jax.shard_map(
        on_device,
        mesh=mesh,
        in_specs=placed,
        out_specs=(P("ctx", "dp"), P("ctx", None), P("dp", "ctx"), P(("dp", "ctx"), None)),
        check_vma=False,
    )
```

time: 2010 us -> 159 us (0.08)
  waiting for transfers between devices: 1550 us -> 0 us
  blocking collectives: 192 us -> 0 us
  Pallas kernels: 0 us -> 153 us
  other arithmetic: 130 us -> 0 us
  matrix products: 77.5 us -> 0 us
  local copies, waits for them, and re-layouts: 37.6 us -> 3.04 us
    all_gather x2 -> x0, waiting for transfers between devices: 1010 us -> none  [carried_in(): gathered = jax.tree.map(lambda a: lax.all_gather(a, axis), part)]
    unnamed x5 -> x0, waiting for transfers between devices: 362 us -> none
    unnamed x1 -> x0, blocking collectives: 192 us -> none
    psum x1 -> x0, waiting for transfers between devices: 174 us -> none  [on_device(): lax.psum((mix_stack, ingoing, outgoing), 'dp')]
    pallas_call x0 -> x4, Pallas kernels: none -> 153 us  [the longest x1 79.3 us: on_device(): pl.pallas_call(carry_kernel, out_shape=(plain, plain), in_specs=[VMEM] *...]
    add x80 -> x0, other arithmetic: 101 us -> none  [the longest x63 91.2 us: link_states(): latter[0][:, None, None] * earlier[1] + latter[1]]
    dot_general x51 -> x0, matrix products: 77.5 us -> none  [the longest x8 14.2 us: one_group(): jnp.einsum('thp,shp->hts', grad_group, conv_group, preferred_element_type...]
  transfers between devices with their start and end apart: 4 -> 0, of which waited for: 4 -> 0; matrix products, arithmetic and copies ran while one was open for 1% -> 0% of each run, Pallas kernels for 0% -> 0%
where the time goes in v1:
time: 159 us; the launch traced here: 157 us
  Pallas kernels  153 us (96%)
  local copies, waits for them, and re-layouts  3.04 us (2%)
    pallas_call x1, Pallas kernels, on_device(): pl.pallas_call(carry_kernel, out_shape=(plain, plain), in_specs=[VMEM] *...  79.3 us
    pallas_call x1, Pallas kernels, on_device(): pl.pallas_call(functools.partial(weight_kernel, 1.0 / math.sqrt(toks * la...  48.8 us
    pallas_call x1, Pallas kernels, on_device(): pl.pallas_call(block_kernel, out_shape=(jax.ShapeDtypeStruct((toks, colum...  19.3 us
    pallas_call x1, Pallas kernels, on_device(): pl.pallas_call(summary_kernel, out_shape=(packed, packed), in_specs=[VMEM...  5.93 us

profile of v1, /device:TPU:2, one launch (start us, length us, event | category | flops | bytes accessed | tf_op | source)
XLA Modules:
  0.0 157.1 jit_solution(8163308633886273164)
XLA Ops:
  0.6 5.9 %summary.1 = (f32[16,136,128]{2,1,0:T(8,128)}, f32[16,136,128]{2,1,0:T(8,128)}) custom-call(bf16[256,2048]{1,0:T(8,128)(2,1)} %conv.3, bf16[256,2048]{1,0:T(8,128)(2,1)} %grad.3, bf16[256,256]{1,0:T(8,128)(2,1)} %maps.3, f32[32,256]{1,0:T(8,128)} %decay.3), custom_call_target="tpu_custom_call" | custom-call | tf_op jit(solution)/shard_map/summary/pallas_call | solution.py:452
  6.6 79.3 %carry.1 = (f32[16,128,128]{2,1,0:T(8,128)}, f32[16,128,128]{2,1,0:T(8,128)}) custom-call(f32[16,136,128]{2,1,0:T(8,128)} %get-tuple-element.13.ahead, f32[16,136,128]{2,1,0:T(8,128)} %get-tuple-element.14.behind), custom_call_target="tpu_custom_call" | custom-call | tf_op jit(solution)/shard_map/carry/pallas_call | solution.py:460
  85.9 19.3 %blocks.1 = (bf16[256,2048]{1,0:T(8,128)(2,1)}, f32[32,256]{1,0:T(8,128)}, f32[256,256]{1,0:T(8,128)}) custom-call(bf16[256,2048]{1,0:T(8,128)(2,1)} %conv.3, bf16[256,2048]{1,0:T(8,128)(2,1)} %grad.3, bf16[256,256]{1,0:T(8,128)(2,1)} %maps.3, f32[32,256]{1,0:T(8,128)} %decay.3, f32[16,128,128]{2,1,0:T(8,128)} %get-tuple-element.15.start, ...), custom_call_target="tpu_custom_call" | custom-call | tf_op jit(solution)/shard_map/blocks/pallas_call | solution.py:484
  105.2 48.8 %weight.1 = (f32[256,256]{1,0:T(8,128)}, f32[32,256]{1,0:T(8,128)}) custom-call(f32[256,256]{1,0:T(8,128)} %get-tuple-element.18.part, bf16[256,2048]{1,0:T(8,128)(2,1)} %layer.1), custom_call_target="tpu_custom_call" | custom-call | tf_op jit(solution)/shard_map/weight/pallas_call | solution.py:507
  154.1 1.7 %copy.11 = f32[256,256]{1,0:T(8,128)} copy(f32[256,256]{1,0:T(8,128)} %get-tuple-element.27) | data formatting | bytes 524288
  155.7 1.4 copy.12

commit v2 on v0

v2 whole, which is shorter than its diff:
```python
import functools
import math

import jax
import jax.numpy as jnp
from jax import lax
from jax.experimental import pallas as pl
from jax.experimental.pallas import tpu as pltpu
from jax.sharding import PartitionSpec as P

BLOCK = 128
HEAD = 64
STATE = 128
PAIR = 2 * HEAD
ROWS = PAIR + 8
Z_SIZE = 8
Y_SIZE = 4
MESH = pl.DeviceIdType.MESH
F32 = jnp.float32
BF16 = jnp.bfloat16
HIGHEST = lax.Precision.HIGHEST
NT = (((1,), (1,)), ((), ()))
TN = (((0,), (0,)), ((), ()))
NN = (((1,), (0,)), ((), ()))
VMEM = pl.BlockSpec(memory_space=pltpu.VMEM)
LIMIT = 56 * 1024 * 1024


def dot(a, b, dims=NN, precision=None):
    return lax.dot_general(a, b, dims, precision=precision, preferred_element_type=F32)


def iota(shape, axis):
    return lax.broadcasted_iota(jnp.int32, shape, axis)


def two_parts(values):
    high = values.astype(BF16)
    return high, (values - high.astype(F32)).astype(BF16)


def head_lanes(first_head, head_count, columns, width):
    shape = (head_count, columns)
    return (iota(shape, 0) == first_head + iota(shape, 1) // width).astype(BF16)


def widen(parts, lanes):
    return dot(parts[0], lanes) + dot(parts[1], lanes)


def place():
    dp, ctx = lax.axis_index("dp"), lax.axis_index("ctx")
    return dp, ctx // (2 * Z_SIZE), (ctx // 2) % Z_SIZE, ctx % 2


def device(dp, y, z, x):
    return (dp, (y * Z_SIZE + z) * 2 + x)


def remote(src, dst, send, recv, target):
    return pltpu.make_async_remote_copy(
        src_ref=src, dst_ref=dst, send_sem=send, recv_sem=recv, device_id=target, device_id_type=MESH
    )


def per_head(tile, values):
    return jnp.concatenate([values[:HEAD] * tile[0:1], values[HEAD:] * tile[4:5]], axis=0)


def order(step):
    odd = step % 2
    return Z_SIZE // 2 + (step // 2) * (1 - odd) - ((step + 1) // 2) * odd


def kernel(
    scale, z_rows,
    conv, grad, maps, decay, layer, grad_conv, grad_maps, grad_decay, weight,
    own, x_in, t_out, z_in, y_in, before, back_out, back_in, x_out, result,
    cum_rows, total_rows, change, ends, mix, flow, wide, weighed, inner_out, finals, backs, states,
    part, gathered, total, flipped, by_y0, by_y1, by_z,
    ry_in0, ry_in1, rz_in, ry_sum0, ry_sum1, rz_sum, rz_late0, rz_late1, ry_late, rx_own, rx_in,
    x_send, x_recv, z_send, z_recv, y_send, y_recv, b_send, b_recv, r_send, r_recv,
    p_send, p_recv, g_send, g_recv, ry_send, ry_recv, rz_send, rz_recv,
    rzl_send, rzl_recv, ryl_send, ryl_recv, rx_send, rx_recv,
):
    dp, y, z, x = place()
    other = device(dp, y, z, 1 - x)

    def z_at(k):
        return device(dp, y, (z + k) % Z_SIZE, x)

    def y_at(m):
        return device(dp, (y + m) % Y_SIZE, z, x)

    def p_at(m):
        return device((dp + m) % 4, y, z, x)

    partners = [other] + [z_at(k) for k in range(1, Z_SIZE)]
    partners += [y_at(m) for m in range(1, Y_SIZE)] + [p_at(m) for m in range(1, 4)]
    barrier = pltpu.get_barrier_semaphore()
    for partner in partners:
        pl.semaphore_signal(barrier, inc=1, device_id=partner, device_id_type=MESH)

    heads, toks = decay.shape
    count = toks // BLOCK
    width = 4 * HEAD
    square = (BLOCK, BLOCK)
    blocks = [slice(block * BLOCK, (block + 1) * BLOCK) for block in range(count)]


    def x_copy(way, k):
        piece = (z + k) % Z_SIZE
        return remote(
            own.at[way, (1 - x) * Z_SIZE + piece], x_in.at[way, piece],
            x_send.at[way, k], x_recv.at[way, k], other,
        )

    def z_copy(way, k):
        return remote(t_out.at[way, k], z_in.at[way, k], z_send.at[way, k], z_recv.at[way, k], z_at(k))

    def y_copy(way, m):
        return remote(y_in.at[way, 0], y_in.at[way, m], y_send.at[way, m], y_recv.at[way, m], y_at(m))

    def b_copy(way, k):
        return remote(
            back_out.at[way, k], back_in.at[way, k], b_send.at[way, k], b_recv.at[way, k], z_at(k)
        )

    def r_copy(way, k):
        piece = x * Z_SIZE + (z + Z_SIZE - k) % Z_SIZE
        return remote(
            x_out.at[way, k], result.at[way, piece], r_send.at[way, k], r_recv.at[way, k], other
        )


    decays = decay[...]
    lower_all = (iota((toks, toks), 1) <= iota((toks, toks), 0)).astype(F32)
    cum_all = dot(lower_all, decays, NT, HIGHEST)
    factors = (two_parts(jnp.exp(cum_all[toks - 1 : toks, :] - cum_all)), two_parts(jnp.exp(cum_all)))
    sources = (conv, grad)
    total_all = jnp.exp(dot(decays, jnp.ones((toks, STATE), F32), NN, HIGHEST))
    expand = (iota((heads * 4, heads), 0) // 4 == iota((heads * 4, heads), 1)).astype(F32)
    tiles = dot(expand, total_all, NN, HIGHEST).reshape(heads // 2, 8, STATE)
    for way in range(2):
        own[way, :, PAIR:, :] = tiles

    def summarize(way, half):
        chunk = 8 * HEAD
        for piece in range(heads // 2 * HEAD // chunk):
            first = half * (heads // 2 * HEAD) + piece * chunk
            columns = pl.ds(pl.multiple_of(first, chunk), chunk)
            lanes = head_lanes(half * (heads // 2) + piece * 8, heads, chunk, HEAD)
            weighted = (widen(factors[way], lanes) * sources[way][:, columns].astype(F32)).astype(BF16)
            made = dot(weighted, maps[:, way * STATE : (way + 1) * STATE], TN)
            own[way, pl.ds(half * Z_SIZE + piece * 4, 4), :PAIR, :] = made.reshape(4, PAIR, STATE)

    summarize(0, 1 - x)
    pl.semaphore_wait(barrier, len(partners))
    for step in range(Z_SIZE):
        x_copy(0, order(step)).start()
    summarize(1, 1 - x)
    for step in range(Z_SIZE):
        x_copy(1, order(step)).start()
    summarize(0, x)
    summarize(1, x)


    causal = iota(square, 1) <= iota(square, 0)
    lower = causal.astype(F32)
    cum_parts, to_end, from_start, scores = [], [], [], []
    for block in range(count):
        rows = blocks[block]
        local = decay[:, rows]
        cum = dot(lower, local, NT, HIGHEST)
        high, middle = two_parts(cum)
        low = (cum - high.astype(F32) - middle.astype(F32)).astype(BF16)
        cum_parts.append((high, middle, low))
        to_end.append(two_parts(jnp.exp(cum[BLOCK - 1 : BLOCK, :] - cum)))
        from_start.append(two_parts(jnp.exp(cum)))
        cum_rows[block] = jnp.broadcast_to(dot(local, lower, NT, HIGHEST)[:, None, :], (heads, 8, BLOCK))
        whole = jnp.exp(dot(local, jnp.ones((BLOCK, STATE), F32), NN, HIGHEST))
        total_rows[block] = jnp.broadcast_to(whole[:, None, :], (heads, 8, STATE))
        scores.append(dot(maps[rows, STATE:], maps[rows, :STATE], NT))
    change[...] = jnp.zeros_like(change)
    mix[...] = jnp.zeros_like(mix)
    flow[...] = jnp.zeros_like(flow)

    def inside(index):
        columns = pl.ds(pl.multiple_of(index * width, width), width)
        pair_slices = pl.ds(index * 2, 2)
        lanes = head_lanes(index * 4, heads, width, HEAD)
        broad = head_lanes(index * 4, heads, 4 * BLOCK, BLOCK)
        in_first = iota((BLOCK, PAIR), 1) < HEAD
        for block in range(count):
            rows = blocks[block]
            xs, gs = conv[rows, columns], grad[rows, columns]
            te, fs = widen(to_end[block], lanes), widen(from_start[block], lanes)
            wide[0, rows, columns] = fs
            wide[1, rows, columns] = te
            xw = (te * xs.astype(F32)).astype(BF16)
            gw = (fs * gs.astype(F32)).astype(BF16)
            weighed[0, rows, columns] = gw
            weighed[1, rows, columns] = xw
            finals[block, pair_slices] = dot(xw, maps[rows, :STATE], TN).reshape(2, PAIR, STATE)
            if block:
                backs[block - 1, pair_slices] = dot(gw, maps[rows, STATE:], TN).reshape(2, PAIR, STATE)
            column = sum(dot(piece, broad) for piece in cum_parts[block])
            y_parts, d_parts, mixed = [], [], None
            for pair in range(2):
                lane = slice(pair * PAIR, (pair + 1) * PAIR)
                x_pair, g_pair = xs[:, lane], gs[:, lane]
                zero = jnp.zeros_like(x_pair)
                x_own = [jnp.where(in_first, x_pair, zero), jnp.where(in_first, zero, x_pair)]
                g_own = [jnp.where(in_first, g_pair, zero), jnp.where(in_first, zero, g_pair)]
                weights = []
                for one in range(2):
                    head = 2 * pair + one
                    col = column[:, head * BLOCK : (head + 1) * BLOCK].reshape(16, 8, BLOCK)
                    gap = (col - cum_rows[block, index * 4 + head][None]).reshape(square)
                    falls = jnp.exp(jnp.where(causal, gap, -1e30))
                    term = falls * dot(g_own[one], x_pair, NT)
                    weights.append((falls * scores[block]).astype(BF16))
                    mixed = term if mixed is None else mixed + term
                y_parts.append(dot(jnp.concatenate(weights, axis=1), jnp.concatenate(x_own, axis=0)))
                d_parts.append(dot(jnp.concatenate(weights, axis=0), jnp.concatenate(g_own, axis=0), TN))
            mix[block] += mixed
            inner_out[0, rows, columns] = jnp.concatenate(y_parts, axis=1)
            inner_out[1, rows, columns] = jnp.concatenate(d_parts, axis=1)


    def join(way, step):
        k = order(step)
        first = x == way
        x_copy(way, k).wait_recv()
        piece = (z + k) % Z_SIZE
        mine = own[way, x * Z_SIZE + piece]
        theirs = x_in[way, piece]
        early = jnp.where(first, mine, theirs)
        late = jnp.where(first, theirs, mine)
        t_out[way, k, :PAIR] = per_head(late[PAIR:], early[:PAIR]) + late[:PAIR]
        t_out[way, k, PAIR:] = early[PAIR:] * late[PAIR:]

        @pl.when(step < Z_SIZE - 1)
        def _():
            z_copy(way, k).start()

    def scan(way):
        for step in range(Z_SIZE - 1):
            z_copy(way, order(step)).wait_recv()
        z_in[way, 0] = t_out[way, 0]
        state = jnp.zeros((PAIR, STATE), F32)
        fade = jnp.ones((8, STATE), F32)
        for step in range(Z_SIZE):
            at = Z_SIZE - 1 - step if way else step
            slot = (z + Z_SIZE - at) % Z_SIZE
            out = (at + Z_SIZE - z) % Z_SIZE
            before[way, out, :PAIR] = state
            before[way, out, PAIR:] = fade
            tile = z_in[way, slot, PAIR:]
            state = per_head(tile, state) + z_in[way, slot, :PAIR]
            fade = fade * tile
        y_in[way, 0, :PAIR] = state
        y_in[way, 0, PAIR:] = fade
        for m in (2, 1, 3):
            y_copy(way, m).start()

    def spread(way):
        for m in range(1, Y_SIZE):
            y_copy(way, m).wait_recv()
        state = jnp.zeros((PAIR, STATE), F32)
        for step in range(Y_SIZE):
            at = Y_SIZE - 1 - step if way else step
            slot = (y + Y_SIZE - at) % Y_SIZE
            counts = (at > y) if way else (at < y)
            new = per_head(y_in[way, slot, PAIR:], state) + y_in[way, slot, :PAIR]
            state = jnp.where(counts, new, state)
        for step in range(Z_SIZE):
            k = order(step)
            target = back_out.at[way, k] if k else back_in.at[way, 0]
            target[...] = before[way, k, :PAIR] + per_head(before[way, k, PAIR:], state)
            if k:
                b_copy(way, k).start()

    def hand_on(way, step):
        k = order(Z_SIZE - 1 - step)
        first = x == way

        @pl.when(step > 0)
        def _():
            b_copy(way, k).wait_recv()

        piece = (z + Z_SIZE - k) % Z_SIZE
        early = back_in[way, k]
        left = jnp.where(first, own[way, x * Z_SIZE + piece], x_in[way, piece])
        late = per_head(left[PAIR:], early) + left[:PAIR]
        x_out[way, k] = jnp.where(first, late, early)
        result[way, x * Z_SIZE + piece] = jnp.where(first, early, late)
        r_copy(way, k).start()


    def fade_rows(block, index, state):
        tiles = total_rows[block, pl.ds(index * 2, 2)][:, None]
        return (state.reshape(2, 8, 8, STATE) * tiles).reshape(PAIR, STATE)

    def add_change(block, index, product):
        lanes = head_lanes(index * 2, heads, PAIR, HEAD)
        high, low = two_parts(product)
        change[block] += dot(lanes, high, NT) + dot(lanes, low, NT)

    def with_start(index):
        columns = pl.ds(pl.multiple_of(index * PAIR, PAIR), PAIR)
        state = result[0, index]
        for block in range(count):
            rows = blocks[block]
            low = state.astype(BF16)
            flow[0, block] += dot(weighed[0, rows, columns], low)
            outputs = inner_out[0, rows, columns] + wide[0, rows, columns] * dot(maps[rows, STATE:], low, NT)
            add_change(block, index, grad[rows, columns].astype(F32) * outputs)
            state = fade_rows(block, index, state) + finals[block, index]
            states[block, index] = state

    def with_finish(index):
        columns = pl.ds(pl.multiple_of(index * PAIR, PAIR), PAIR)
        state = result[1, index]
        for block in reversed(range(count)):
            rows = blocks[block]
            ends[block, pl.ds(index * 2, 2)] = jnp.sum(
                (state * states[block, index]).reshape(2, 8, 8, STATE), axis=1
            )
            low = state.astype(BF16)
            flow[1, block] += dot(weighed[1, rows, columns], low)
            inputs = inner_out[1, rows, columns] + wide[1, rows, columns] * dot(maps[rows, :STATE], low, NT)
            grad_conv[rows, columns] = inputs.astype(BF16)
            add_change(block, index, conv[rows, columns].astype(F32) * -inputs)
            if block:
                state = fade_rows(block, index, state) + backs[block - 1, index]


    share = toks // 4
    mine = pl.ds(pl.multiple_of(dp * share, share), share)

    def p_copy(half, m):
        rows = pl.ds(pl.multiple_of((dp + m) % 4 * share, share), share)
        return remote(
            part.at[half, rows], gathered.at[half, m], p_send.at[half, m], p_recv.at[half, m], p_at(m)
        )

    def g_copy(half, m):
        return remote(
            total.at[half, mine], total.at[half, mine], g_send.at[half, m], g_recv.at[half, m], p_at(m)
        )

    def sum_begin(half):
        for block in range(count):
            rows = blocks[block]
            if half:
                made = dot(mix[block], maps[rows, STATE:].astype(F32), TN, HIGHEST)
            else:
                made = dot(mix[block], maps[rows, :STATE].astype(F32), NN, HIGHEST)
            part[half, rows] = made + flow[half, block]
        for m in range(1, 4):
            p_copy(half, m).start()

    def sum_middle(half):
        for m in range(1, 4):
            p_copy(half, m).wait_recv()
        total[half, mine] = part[half, mine] + gathered[half, 1] + gathered[half, 2] + gathered[half, 3]
        for m in range(1, 4):
            g_copy(half, m).start()

    def sum_end(half):
        for m in range(1, 4):
            g_copy(half, m).wait_recv()
        made = total[half]
        grad_maps[:, (1 - half) * STATE : (2 - half) * STATE] = made
        return made.astype(BF16)


    by_y, ry_in, ry_sum, rz_late = (by_y0, by_y1), (ry_in0, ry_in1), (ry_sum0, ry_sum1), (rz_late0, rz_late1)
    splits = (0, z_rows)

    def ry_copy(half, m):
        return remote(
            by_y[half].at[(y + m) % Y_SIZE], ry_in[half].at[m], ry_send.at[half, m], ry_recv.at[half, m], y_at(m)
        )

    def rzl_copy(half, k):
        return remote(
            ry_sum[half].at[(z + k) % Z_SIZE], rz_late[half].at[k],
            rzl_send.at[half, k], rzl_recv.at[half, k], z_at(k),
        )

    def rz_copy(k):
        return remote(by_z.at[(z + k) % Z_SIZE], rz_in.at[k], rz_send.at[k], rz_recv.at[k], z_at(k))

    def ryl_copy(m):
        return remote(
            rz_sum.at[(y + m) % Y_SIZE], ry_late.at[m], ryl_send.at[m], ryl_recv.at[m], y_at(m)
        )

    def rx_copy(half):
        return remote(
            rx_own.at[half, 1 - x], rx_in.at[half], rx_send.at[half], rx_recv.at[half], other
        )

    def weigh(half, low):
        cut = splits[half]
        for piece in range(Y_SIZE):
            made = dot(flipped[piece], low) * scale
            made = made.reshape(Z_SIZE, 2, -1, STATE)
            by_y[half][piece] = made[:, :, cut:]
            if cut:
                by_z[:, piece] = made[:, :, :cut]
        if cut:
            for step in range(3):
                rz_copy(order(step)).start()
        for m in (2, 1, 3):
            ry_copy(half, m).start()
        if cut:
            for step in range(3, Z_SIZE - 1):
                rz_copy(order(step)).start()

    def weigh_middle(half):
        for m in range(1, Y_SIZE):
            ry_copy(half, m).wait_recv()
        ry_sum[half][...] = by_y[half][y] + ry_in[half][1] + ry_in[half][2] + ry_in[half][3]
        for step in range(Z_SIZE - 1):
            rzl_copy(half, order(step)).start()

    def weigh_middle_z():
        for k in range(1, Z_SIZE):
            rz_copy(k).wait_recv()
        rz_sum[...] = by_z[z] + sum(rz_in[k] for k in range(1, Z_SIZE))
        for m in (2, 1, 3):
            ryl_copy(m).start()

    def weigh_late(half):
        cut = splits[half]
        if cut:
            for m in range(1, Y_SIZE):
                ryl_copy(m).wait_recv()
            rx_own[half, :, :cut] = rz_sum[y] + sum(ry_late[m] for m in range(1, Y_SIZE))
        for k in range(1, Z_SIZE):
            rzl_copy(half, k).wait_recv()
        rx_own[half, :, cut:] = ry_sum[half][z] + sum(rz_late[half][k] for k in range(1, Z_SIZE))
        rx_copy(half).start()

    def weigh_end(half):
        rx_copy(half).wait_recv()
        weight[:, (1 - half) * STATE : (2 - half) * STATE] = rx_own[half, x] + rx_in[half]


    span = layer.shape[1] // Y_SIZE
    for piece in range(Y_SIZE):
        flipped[piece] = layer[:, piece * span : (piece + 1) * span].T

    def joins(turn, _):
        way, step = turn // 4, turn % 4 * 2
        join(way, step)
        join(way, step + 1)
        inside(turn)

        @pl.when(turn == 5)
        def _():
            scan(0)

        return 0

    lax.fori_loop(0, Z_SIZE, joins, 0)
    spread(0)

    def starts(turn, _):
        way, step = turn // Z_SIZE, turn % Z_SIZE
        hand_on(way, step)

        @pl.when(turn >= Z_SIZE)
        def _():
            r_copy(0, order(Z_SIZE - 1 - step)).wait_recv()

        piece = (z + Z_SIZE - order(Z_SIZE - 1 - step)) % Z_SIZE
        half = x + way * (1 - 2 * x)
        with_start(half * Z_SIZE + piece)

        @pl.when(turn == 2)
        def _():
            scan(1)

        @pl.when(turn == 4)
        def _():
            spread(1)

        return 0

    lax.fori_loop(0, 2 * Z_SIZE, starts, 0)
    sum_begin(0)

    def finishes(turn, _):
        way, step = turn // Z_SIZE, turn % Z_SIZE

        @pl.when(turn >= Z_SIZE)
        def _():
            r_copy(1, order(Z_SIZE - 1 - step)).wait_recv()

        piece = (z + Z_SIZE - order(Z_SIZE - 1 - step)) % Z_SIZE
        half = x + way * (1 - 2 * x)
        with_finish(half * Z_SIZE + piece)

        @pl.when(turn == Z_SIZE - 1)
        def _():
            sum_middle(0)

        return 0

    lax.fori_loop(0, 2 * Z_SIZE, finishes, 0)
    sum_begin(1)
    low = sum_end(0)
    weigh(0, low)
    sum_middle(1)
    low = sum_end(1)
    weigh(1, low)
    for block in range(count):
        end_term = jnp.sum(jnp.sum(ends[block], axis=1), axis=1, keepdims=True)
        at_last = iota((heads, BLOCK), 1) == BLOCK - 1
        changes = change[block] + jnp.where(at_last, end_term, 0.0)
        grad_decay[:, blocks[block]] = dot(changes, lower, NN, HIGHEST)
    weigh_middle(0)
    weigh_middle_z()
    weigh_middle(1)
    weigh_late(0)
    weigh_late(1)
    weigh_end(0)
    weigh_end(1)

    for way in range(2):
        for k in range(Z_SIZE):
            x_copy(way, k).wait_send()
            r_copy(way, k).wait_send()
            if k:
                z_copy(way, k).wait_send()
                b_copy(way, k).wait_send()
                rzl_copy(way, k).wait_send()
                if way:
                    rz_copy(k).wait_send()
        for m in range(1, 4):
            y_copy(way, m).wait_send()
            p_copy(way, m).wait_send()
            g_copy(way, m).wait_send()
            ry_copy(way, m).wait_send()
            if way:
                ryl_copy(m).wait_send()
        rx_copy(way).wait_send()


def dma(*shape):
    return pltpu.SemaphoreType.DMA(shape)


def on_device(layer_input, conv_output, state_maps, log_decay, out_grad):
    toks, columns = conv_output.shape
    heads = log_decay.shape[0]
    slices = heads // 2
    count = toks // BLOCK
    tile = columns // (Y_SIZE * Z_SIZE * 2)
    z_rows = 8
    late = tile - z_rows

    def floats(*shape):
        return pltpu.VMEM(shape, F32)

    grad_conv, grad_maps, grad_decay, grad_weight = pl.pallas_call(
        functools.partial(kernel, 1.0 / math.sqrt(toks * lax.axis_size("ctx")), z_rows),
        out_shape=(
            jax.ShapeDtypeStruct((toks, columns), BF16),
            jax.ShapeDtypeStruct((toks, 2 * STATE), F32),
            jax.ShapeDtypeStruct((heads, toks), F32),
            jax.ShapeDtypeStruct((tile, 2 * STATE), F32),
        ),
        in_specs=[VMEM] * 5,
        out_specs=(VMEM,) * 4,
        scratch_shapes=[
            floats(2, slices, ROWS, STATE),
            floats(2, Z_SIZE, ROWS, STATE),
            floats(2, Z_SIZE, ROWS, STATE),
            floats(2, Z_SIZE, ROWS, STATE),
            floats(2, Y_SIZE, ROWS, STATE),
            floats(2, Z_SIZE, ROWS, STATE),
            floats(2, Z_SIZE, PAIR, STATE),
            floats(2, Z_SIZE, PAIR, STATE),
            floats(2, Z_SIZE, PAIR, STATE),
            floats(2, slices, PAIR, STATE),
            floats(count, heads, 8, BLOCK),
            floats(count, heads, 8, STATE),
            floats(count, heads, BLOCK),
            floats(count, heads, 8, STATE),
            floats(count, BLOCK, BLOCK),
            floats(2, count, BLOCK, STATE),
            floats(2, toks, columns),
            pltpu.VMEM((2, toks, columns), BF16),
            floats(2, toks, columns),
            floats(count, slices, PAIR, STATE),
            floats(max(count - 1, 1), slices, PAIR, STATE),
            floats(count, slices, PAIR, STATE),
            floats(2, toks, STATE),
            floats(2, 4, toks // 4, STATE),
            floats(2, toks, STATE),
            pltpu.VMEM((Y_SIZE, columns // Y_SIZE, toks), BF16),
            floats(Y_SIZE, Z_SIZE, 2, tile, STATE),
            floats(Y_SIZE, Z_SIZE, 2, late, STATE),
            floats(Z_SIZE, Y_SIZE, 2, z_rows, STATE),
            floats(Y_SIZE, Z_SIZE, 2, tile, STATE),
            floats(Y_SIZE, Z_SIZE, 2, late, STATE),
            floats(Z_SIZE, Y_SIZE, 2, z_rows, STATE),
            floats(Z_SIZE, 2, tile, STATE),
            floats(Z_SIZE, 2, late, STATE),
            floats(Y_SIZE, 2, z_rows, STATE),
            floats(Z_SIZE, 2, tile, STATE),
            floats(Z_SIZE, 2, late, STATE),
            floats(Y_SIZE, 2, z_rows, STATE),
            floats(2, 2, tile, STATE),
            floats(2, tile, STATE),
            dma(2, Z_SIZE), dma(2, Z_SIZE), dma(2, Z_SIZE), dma(2, Z_SIZE),
            dma(2, Y_SIZE), dma(2, Y_SIZE), dma(2, Z_SIZE), dma(2, Z_SIZE),
            dma(2, Z_SIZE), dma(2, Z_SIZE),
            dma(2, 4), dma(2, 4), dma(2, 4), dma(2, 4),
            dma(2, Y_SIZE), dma(2, Y_SIZE), dma(Z_SIZE), dma(Z_SIZE),
            dma(2, Z_SIZE), dma(2, Z_SIZE), dma(Y_SIZE), dma(Y_SIZE),
            dma(2), dma(2),
        ],
        compiler_params=pltpu.CompilerParams(
            collective_id=0, has_side_effects=True, vmem_limit_bytes=LIMIT
        ),
        name="backward",
    )(conv_output, out_grad, state_maps, log_decay, layer_input)
    return (grad_conv, grad_maps, grad_decay, grad_weight)


def solution(mesh):
    placed = (P("ctx", "dp"), P("ctx", "dp"), P("ctx", None), P("dp", "ctx"), P("ctx", "dp"))
    return jax.shard_map(
        on_device,
        mesh=mesh,
        in_specs=placed,
        out_specs=(P("ctx", "dp"), P("ctx", None), P("dp", "ctx"), P(("dp", "ctx"), None)),
        check_vma=False,
    )
```

time: 2010 us -> 128 us (0.06)
  waiting for transfers between devices: 1550 us -> 0 us
  blocking collectives: 192 us -> 0 us
  other arithmetic: 130 us -> 0 us
  Pallas kernels: 0 us -> 121 us
  matrix products: 77.5 us -> 0 us
  local copies, waits for them, and re-layouts: 37.6 us -> 4.49 us
    all_gather x2 -> x0, waiting for transfers between devices: 1010 us -> none  [carried_in(): gathered = jax.tree.map(lambda a: lax.all_gather(a, axis), part)]
    unnamed x5 -> x0, waiting for transfers between devices: 362 us -> none
    unnamed x1 -> x0, blocking collectives: 192 us -> none
    psum x1 -> x0, waiting for transfers between devices: 174 us -> none  [on_device(): lax.psum((mix_stack, ingoing, outgoing), 'dp')]
    pallas_call x0 -> x1, Pallas kernels: none -> 121 us  [on_device(): pl.pallas_call(functools.partial(kernel, 1.0 / math.sqrt(toks * lax.axis_...]
    add x80 -> x0, other arithmetic: 101 us -> none  [the longest x63 91.2 us: link_states(): latter[0][:, None, None] * earlier[1] + latter[1]]
    dot_general x51 -> x0, matrix products: 77.5 us -> none  [the longest x8 14.2 us: one_group(): jnp.einsum('thp,shp->hts', grad_group, conv_group, preferred_element_type...]
  transfers between devices with their start and end apart: 4 -> 0, of which waited for: 4 -> 0; matrix products, arithmetic and copies ran while one was open for 1% -> 0% of each run, Pallas kernels for 0% -> 0%
where the time goes in v2:
time: 128 us; the launch traced here: 126 us
  Pallas kernels  121 us (95%)
  local copies, waits for them, and re-layouts  4.49 us (4%)
    pallas_call x1, Pallas kernels, on_device(): pl.pallas_call(functools.partial(kernel, 1.0 / math.sqrt(toks * lax.axis_...  121 us
    unnamed x10, local copies, waits for them, and re-layouts  4.49 us

profile of v2, /device:TPU:2, one launch (start us, length us, event | category | flops | bytes accessed | tf_op | source)
XLA Modules:
  0.0 125.9 jit_solution(532526959409348956)
XLA Ops:
  0.6 120.7 %backward.1 = (bf16[256,2048]{1,0:T(8,128)(2,1)}, f32[256,256]{1,0:T(8,128)}, f32[32,256]{1,0:T(8,128)}, f32[32,256]{1,0:T(8,128)}) custom-call(bf16[256,2048]{1,0:T(8,128)(2,1)} %conv.1, bf16[256,2048]{1,0:T(8,128)(2,1)} %grad.1, bf16[256,256]{1,0:T(8,128)(2,1)} %maps.1, f32[32,256]{1,0:T(8,128)} %decay.1, bf16[256,2048]{1,0:T(8,128)(2,1)} %layer.1), custom_call_target="tpu_custom_call" | custom-call | tf_op jit(solution)/shard_map/backward/pallas_call | solution.py:570
  121.4 0.0 copy-start
  121.4 2.3 %copy.13 = bf16[256,2048]{1,0:T(8,128)(2,1)} copy(bf16[256,2048]{1,0:T(8,128)(2,1)} %get-tuple-element.8) | data formatting | bytes 2097152
  123.7 0.0 copy-done
  123.7 0.0 copy-start.2
  123.7 0.7 copy.14
  124.4 0.1 copy-done.2
  124.5 0.0 copy-start.1
  124.5 0.6 copy.15
  125.1 0.2 copy-done.1
  125.2 0.6 copy.16
Async XLA Ops:
  121.4 2.4 %copy-start = (f32[256,256]{1,0:T(8,128)S(1)}, f32[256,256]{1,0:T(8,128)}, u32[]{:S(2)}) copy-start(f32[256,256]{1,0:T(8,128)} %get-tuple-element.9) | copy-start | bytes 786436
  123.7 0.8 copy-start.2
  124.5 0.8 copy-start.1

commit v3 on v2

--- a/solution.py
+++ b/solution.py
@@ -12,7 +12,7 @@
 HEAD = 64
 STATE = 128
 PAIR = 2 * HEAD
-ROWS = PAIR + 8
+CHUNKS = 4
 Z_SIZE = 8
 Y_SIZE = 4
 MESH = pl.DeviceIdType.MESH
@@ -63,8 +63,8 @@
     )
 
 
-def per_head(tile, values):
-    return jnp.concatenate([values[:HEAD] * tile[0:1], values[HEAD:] * tile[4:5]], axis=0)
+def pick(tile, part):
+    return jnp.where(part == 0, tile[0:1], tile[4:5])
 
 
 def order(step):
@@ -76,10 +76,12 @@
     scale, z_rows,
     conv, grad, maps, decay, layer, grad_conv, grad_maps, grad_decay, weight,
     own, x_in, t_out, z_in, y_in, before, back_out, back_in, x_out, result,
+    d_own, d_x, d_t, d_z, d_y, d_before,
     cum_rows, total_rows, change, ends, mix, flow, wide, weighed, inner_out, finals, backs, states,
     part, gathered, total, flipped, by_y0, by_y1, by_z,
     ry_in0, ry_in1, rz_in, ry_sum0, ry_sum1, rz_sum, rz_late0, rz_late1, ry_late, rx_own, rx_in,
     x_send, x_recv, z_send, z_recv, y_send, y_recv, b_send, b_recv, r_send, r_recv,
+    dx_send, dx_recv, dz_send, dz_recv, dy_send, dy_recv,
     p_send, p_recv, g_send, g_recv, ry_send, ry_recv, rz_send, rz_recv,
     rzl_send, rzl_recv, ryl_send, ryl_recv, rx_send, rx_recv,
 ):
@@ -108,29 +110,47 @@
     blocks = [slice(block * BLOCK, (block + 1) * BLOCK) for block in range(count)]
 
 
-    def x_copy(way, k):
-        piece = (z + k) % Z_SIZE
-        return remote(
-            own.at[way, (1 - x) * Z_SIZE + piece], x_in.at[way, piece],
-            x_send.at[way, k], x_recv.at[way, k], other,
-        )
-
-    def z_copy(way, k):
-        return remote(t_out.at[way, k], z_in.at[way, k], z_send.at[way, k], z_recv.at[way, k], z_at(k))
-
-    def y_copy(way, m):
-        return remote(y_in.at[way, 0], y_in.at[way, m], y_send.at[way, m], y_recv.at[way, m], y_at(m))
-
-    def b_copy(way, k):
-        return remote(
-            back_out.at[way, k], back_in.at[way, k], b_send.at[way, k], b_recv.at[way, k], z_at(k)
-        )
-
-    def r_copy(way, k):
+    def head_rows(chunk):
+        return pl.ds(pl.multiple_of(chunk % 2 * HEAD, HEAD), HEAD)
+
+    def x_copy(chunk, k):
+        piece, rows = (z + k) % Z_SIZE, head_rows(chunk)
+        return remote(
+            own.at[chunk // 2, (1 - x) * Z_SIZE + piece, rows], x_in.at[chunk // 2, piece, rows],
+            x_send.at[chunk, k], x_recv.at[chunk, k], other,
+        )
+
+    def z_copy(chunk, k):
+        return remote(
+            t_out.at[chunk, k], z_in.at[chunk, k], z_send.at[chunk, k], z_recv.at[chunk, k], z_at(k)
+        )
+
+    def y_copy(chunk, m):
+        return remote(
+            y_in.at[chunk, 0], y_in.at[chunk, m], y_send.at[chunk, m], y_recv.at[chunk, m], y_at(m)
+        )
+
+    def b_copy(chunk, k):
+        return remote(
+            back_out.at[chunk, k], back_in.at[chunk, k], b_send.at[chunk, k], b_recv.at[chunk, k], z_at(k)
+        )
+
+    def r_copy(chunk, k):
         piece = x * Z_SIZE + (z + Z_SIZE - k) % Z_SIZE
         return remote(
-            x_out.at[way, k], result.at[way, piece], r_send.at[way, k], r_recv.at[way, k], other
-        )
+            x_out.at[chunk, k], result.at[chunk // 2, piece, head_rows(chunk)],
+            r_send.at[chunk, k], r_recv.at[chunk, k], other,
+        )
+
+    def dx_copy():
+        rows = pl.ds((1 - x) * Z_SIZE, Z_SIZE)
+        return remote(d_own.at[rows], d_x, dx_send.at[0], dx_recv.at[0], other)
+
+    def dz_copy(k):
+        return remote(d_t.at[k], d_z.at[k], dz_send.at[k], dz_recv.at[k], z_at(k))
+
+    def dy_copy(m):
+        return remote(d_y.at[0], d_y.at[m], dy_send.at[m], dy_recv.at[m], y_at(m))
 
 
     decays = decay[...]
@@ -140,9 +160,7 @@
     sources = (conv, grad)
     total_all = jnp.exp(dot(decays, jnp.ones((toks, STATE), F32), NN, HIGHEST))
     expand = (iota((heads * 4, heads), 0) // 4 == iota((heads * 4, heads), 1)).astype(F32)
-    tiles = dot(expand, total_all, NN, HIGHEST).reshape(heads // 2, 8, STATE)
-    for way in range(2):
-        own[way, :, PAIR:, :] = tiles
+    d_own[...] = dot(expand, total_all, NN, HIGHEST).reshape(heads // 2, 8, STATE)
 
     def summarize(way, half):
         chunk = 8 * HEAD
@@ -152,15 +170,18 @@
             lanes = head_lanes(half * (heads // 2) + piece * 8, heads, chunk, HEAD)
             weighted = (widen(factors[way], lanes) * sources[way][:, columns].astype(F32)).astype(BF16)
             made = dot(weighted, maps[:, way * STATE : (way + 1) * STATE], TN)
-            own[way, pl.ds(half * Z_SIZE + piece * 4, 4), :PAIR, :] = made.reshape(4, PAIR, STATE)
+            own[way, pl.ds(half * Z_SIZE + piece * 4, 4)] = made.reshape(4, PAIR, STATE)
 
     summarize(0, 1 - x)
     pl.semaphore_wait(barrier, len(partners))
-    for step in range(Z_SIZE):
-        x_copy(0, order(step)).start()
+    dx_copy().start()
+    for chunk in range(2):
+        for step in range(Z_SIZE):
+            x_copy(chunk, order(step)).start()
     summarize(1, 1 - x)
-    for step in range(Z_SIZE):
-        x_copy(1, order(step)).start()
+    for chunk in range(2, CHUNKS):
+        for step in range(Z_SIZE):
+            x_copy(chunk, order(step)).start()
     summarize(0, x)
     summarize(1, x)
 
@@ -228,74 +249,95 @@
             inner_out[1, rows, columns] = jnp.concatenate(d_parts, axis=1)
 
 
-    def join(way, step):
+    def pass_decays():
+        dx_copy().wait_recv()
+        for step in range(Z_SIZE):
+            k = order(step)
+            piece = (z + k) % Z_SIZE
+            target = d_t.at[k] if k else d_z.at[0]
+            target[...] = d_own[x * Z_SIZE + piece] * d_x[piece]
+            if k:
+                dz_copy(k).start()
+
+    def scan_decays():
+        for k in range(1, Z_SIZE):
+            dz_copy(k).wait_recv()
+        for way in range(2):
+            fade = jnp.ones((8, STATE), F32)
+            for step in range(Z_SIZE):
+                at = Z_SIZE - 1 - step if way else step
+                d_before[way, (at + Z_SIZE - z) % Z_SIZE] = fade
+                fade = fade * d_z[(z + Z_SIZE - at) % Z_SIZE]
+        d_y[0] = fade
+        for m in (2, 1, 3):
+            dy_copy(m).start()
+
+    def join(chunk, step):
+        way, part, rows = chunk // 2, chunk % 2, head_rows(chunk)
         k = order(step)
         first = x == way
-        x_copy(way, k).wait_recv()
+        x_copy(chunk, k).wait_recv()
         piece = (z + k) % Z_SIZE
-        mine = own[way, x * Z_SIZE + piece]
-        theirs = x_in[way, piece]
+        mine = own[way, x * Z_SIZE + piece, rows]
+        theirs = x_in[way, piece, rows]
         early = jnp.where(first, mine, theirs)
         late = jnp.where(first, theirs, mine)
-        t_out[way, k, :PAIR] = per_head(late[PAIR:], early[:PAIR]) + late[:PAIR]
-        t_out[way, k, PAIR:] = early[PAIR:] * late[PAIR:]
+        fade = pick(jnp.where(first, d_x[piece], d_own[x * Z_SIZE + piece]), part)
+        t_out[chunk, k] = fade * early + late
 
         @pl.when(step < Z_SIZE - 1)
         def _():
-            z_copy(way, k).start()
-
-    def scan(way):
+            z_copy(chunk, k).start()
+
+    def scan(chunk):
+        way, part = chunk // 2, chunk % 2
         for step in range(Z_SIZE - 1):
-            z_copy(way, order(step)).wait_recv()
-        z_in[way, 0] = t_out[way, 0]
-        state = jnp.zeros((PAIR, STATE), F32)
-        fade = jnp.ones((8, STATE), F32)
+            z_copy(chunk, order(step)).wait_recv()
+        z_in[chunk, 0] = t_out[chunk, 0]
+        state = jnp.zeros((HEAD, STATE), F32)
         for step in range(Z_SIZE):
-            at = Z_SIZE - 1 - step if way else step
+            at = step + way * (Z_SIZE - 1 - 2 * step)
             slot = (z + Z_SIZE - at) % Z_SIZE
-            out = (at + Z_SIZE - z) % Z_SIZE
-            before[way, out, :PAIR] = state
-            before[way, out, PAIR:] = fade
-            tile = z_in[way, slot, PAIR:]
-            state = per_head(tile, state) + z_in[way, slot, :PAIR]
-            fade = fade * tile
-        y_in[way, 0, :PAIR] = state
-        y_in[way, 0, PAIR:] = fade
+            before[chunk, (at + Z_SIZE - z) % Z_SIZE] = state
+            state = pick(d_z[slot], part) * state + z_in[chunk, slot]
+        y_in[chunk, 0] = state
         for m in (2, 1, 3):
-            y_copy(way, m).start()
-
-    def spread(way):
+            y_copy(chunk, m).start()
+
+    def spread(chunk):
+        way, part = chunk // 2, chunk % 2
         for m in range(1, Y_SIZE):
-            y_copy(way, m).wait_recv()
-        state = jnp.zeros((PAIR, STATE), F32)
+            y_copy(chunk, m).wait_recv()
+        state = jnp.zeros((HEAD, STATE), F32)
         for step in range(Y_SIZE):
-            at = Y_SIZE - 1 - step if way else step
+            at = step + way * (Y_SIZE - 1 - 2 * step)
             slot = (y + Y_SIZE - at) % Y_SIZE
-            counts = (at > y) if way else (at < y)
-            new = per_head(y_in[way, slot, PAIR:], state) + y_in[way, slot, :PAIR]
-            state = jnp.where(counts, new, state)
+            counts = (at - y) * (1 - 2 * way) < 0
+            state = jnp.where(counts, pick(d_y[slot], part) * state + y_in[chunk, slot], state)
         for step in range(Z_SIZE):
             k = order(step)
-            target = back_out.at[way, k] if k else back_in.at[way, 0]
-            target[...] = before[way, k, :PAIR] + per_head(before[way, k, PAIR:], state)
+            target = back_out.at[chunk, k] if k else back_in.at[chunk, 0]
+            target[...] = before[chunk, k] + pick(d_before[way, k], part) * state
             if k:
-                b_copy(way, k).start()
-
-    def hand_on(way, step):
+                b_copy(chunk, k).start()
+
+    def hand_on(chunk, step):
+        way, part, rows = chunk // 2, chunk % 2, head_rows(chunk)
         k = order(Z_SIZE - 1 - step)
         first = x == way
 
         @pl.when(step > 0)
         def _():
-            b_copy(way, k).wait_recv()
+            b_copy(chunk, k).wait_recv()
 
         piece = (z + Z_SIZE - k) % Z_SIZE
-        early = back_in[way, k]
-        left = jnp.where(first, own[way, x * Z_SIZE + piece], x_in[way, piece])
-        late = per_head(left[PAIR:], early) + left[:PAIR]
-        x_out[way, k] = jnp.where(first, late, early)
-        result[way, x * Z_SIZE + piece] = jnp.where(first, early, late)
-        r_copy(way, k).start()
+        early = back_in[chunk, k]
+        left = jnp.where(first, own[way, x * Z_SIZE + piece, rows], x_in[way, piece, rows])
+        fade = pick(jnp.where(first, d_own[x * Z_SIZE + piece], d_x[piece]), part)
+        late = fade * early + left
+        x_out[chunk, k] = jnp.where(first, late, early)
+        result[way, x * Z_SIZE + piece, rows] = jnp.where(first, early, late)
+        r_copy(chunk, k).start()
 
 
     def fade_rows(block, index, state):
@@ -450,71 +492,100 @@
         weight[:, (1 - half) * STATE : (2 - half) * STATE] = rx_own[half, x] + rx_in[half]
 
 
+    def done(turn):
+        return jnp.where(turn == 0, 0, jnp.minimum(turn + 1, heads * HEAD // width))
+
+    def joins(turn, _):
+        chunk = turn // 2
+
+        def one_join(step, _):
+            join(chunk, step)
+            return 0
+
+        def one_group(index, _):
+            inside(index)
+            return 0
+
+        lax.fori_loop(turn % 2 * 4, turn % 2 * 4 + 4, one_join, 0)
+        lax.fori_loop(done(turn), done(turn + 1), one_group, 0)
+
+        @pl.when(turn == 1)
+        def _():
+            scan_decays()
+
+        @pl.when(turn == 3)
+        def _():
+            for m in range(1, Y_SIZE):
+                dy_copy(m).wait_recv()
+
+        @pl.when(jnp.logical_and(turn >= 2, turn % 2 == 0))
+        def _():
+            scan(chunk - 1)
+
+        @pl.when(jnp.logical_and(turn >= 3, turn % 2 == 1))
+        def _():
+            spread(chunk - 1)
+
+        return 0
+
+    def nearest(step):
+        return order(Z_SIZE - 1 - step)
+
+    def piece_of(half, step):
+        return half * Z_SIZE + (z + Z_SIZE - nearest(step)) % Z_SIZE
+
+    def first_chunk(step, _):
+        hand_on(0, step)
+        return 0
+
+    def second_chunk(step, _):
+        hand_on(1, step)
+        with_start(piece_of(x, step))
+
+        @pl.when(step == 3)
+        def _():
+            spread(3)
+
+        return 0
+
+    def third_chunk(step, _):
+        hand_on(2, step)
+        r_copy(0, nearest(step)).wait_recv()
+        r_copy(1, nearest(step)).wait_recv()
+        with_start(piece_of(1 - x, step))
+        return 0
+
+    def last_chunk(step, _):
+        hand_on(3, step)
+        with_finish(piece_of(x, step))
+
+        @pl.when(step == 3)
+        def _():
+            sum_middle(0)
+
+        return 0
+
+    def others_last(step, _):
+        r_copy(2, nearest(step)).wait_recv()
+        r_copy(3, nearest(step)).wait_recv()
+        with_finish(piece_of(1 - x, step))
+        return 0
+
+    pass_decays()
+    lax.fori_loop(0, Z_SIZE, joins, 0)
+    lax.fori_loop(0, Z_SIZE, first_chunk, 0)
     span = layer.shape[1] // Y_SIZE
     for piece in range(Y_SIZE):
         flipped[piece] = layer[:, piece * span : (piece + 1) * span].T
-
-    def joins(turn, _):
-        way, step = turn // 4, turn % 4 * 2
-        join(way, step)
-        join(way, step + 1)
-        inside(turn)
-
-        @pl.when(turn == 5)
-        def _():
-            scan(0)
-
-        return 0
-
-    lax.fori_loop(0, Z_SIZE, joins, 0)
-    spread(0)
-
-    def starts(turn, _):
-        way, step = turn // Z_SIZE, turn % Z_SIZE
-        hand_on(way, step)
-
-        @pl.when(turn >= Z_SIZE)
-        def _():
-            r_copy(0, order(Z_SIZE - 1 - step)).wait_recv()
-
-        piece = (z + Z_SIZE - order(Z_SIZE - 1 - step)) % Z_SIZE
-        half = x + way * (1 - 2 * x)
-        with_start(half * Z_SIZE + piece)
-
-        @pl.when(turn == 2)
-        def _():
-            scan(1)
-
-        @pl.when(turn == 4)
-        def _():
-            spread(1)
-
-        return 0
-
-    lax.fori_loop(0, 2 * Z_SIZE, starts, 0)
+    scan(3)
+    lax.fori_loop(0, Z_SIZE, second_chunk, 0)
+    lax.fori_loop(0, Z_SIZE, third_chunk, 0)
     sum_begin(0)
-
-    def finishes(turn, _):
-        way, step = turn // Z_SIZE, turn % Z_SIZE
-
-        @pl.when(turn >= Z_SIZE)
-        def _():
-            r_copy(1, order(Z_SIZE - 1 - step)).wait_recv()
-
-        piece = (z + Z_SIZE - order(Z_SIZE - 1 - step)) % Z_SIZE
-        half = x + way * (1 - 2 * x)
-        with_finish(half * Z_SIZE + piece)
-
-        @pl.when(turn == Z_SIZE - 1)
-        def _():
-            sum_middle(0)
-
-        return 0
-
-    lax.fori_loop(0, 2 * Z_SIZE, finishes, 0)
-    sum_begin(1)
+    lax.fori_loop(0, Z_SIZE, last_chunk, 0)
     low = sum_end(0)
     weigh(0, low)
+    lax.fori_loop(0, Z_SIZE, others_last, 0)
+    sum_begin(1)
     sum_middle(1)
     low = sum_end(1)
     weigh(1, low)
@@ -531,28 +602,43 @@
     weigh_end(0)
     weigh_end(1)
 
-    for way in range(2):
+    dx_copy().wait_send()
+    for chunk in range(CHUNKS):
         for k in range(Z_SIZE):
-            x_copy(way, k).wait_send()
-            r_copy(way, k).wait_send()
+            x_copy(chunk, k).wait_send()
+            r_copy(chunk, k).wait_send()
             if k:
-                z_copy(way, k).wait_send()
-                b_copy(way, k).wait_send()
-                rzl_copy(way, k).wait_send()
-                if way:
-                    rz_copy(k).wait_send()
-        for m in range(1, 4):
-            y_copy(way, m).wait_send()
-            p_copy(way, m).wait_send()
-            g_copy(way, m).wait_send()
-            ry_copy(way, m).wait_send()
-            if way:
-                ryl_copy(m).wait_send()
-        rx_copy(way).wait_send()
+                z_copy(chunk, k).wait_send()
+                b_copy(chunk, k).wait_send()
+        for m in range(1, Y_SIZE):
+            y_copy(chunk, m).wait_send()
+    for k in range(1, Z_SIZE):
+        dz_copy(k).wait_send()
+        rz_copy(k).wait_send()
+        for half in range(2):
+            rzl_copy(half, k).wait_send()
+    for m in range(1, 4):
+        dy_copy(m).wait_send()
+        ryl_copy(m).wait_send()
+        for half in range(2):
+            p_copy(half, m).wait_send()
+            g_copy(half, m).wait_send()
+            ry_copy(half, m).wait_send()
+    for half in range(2):
+        rx_copy(half).wait_send()
 
 
 def dma(*shape):
     return pltpu.SemaphoreType.DMA(shape)
+
+
+def hand_out_kernel(a, b, c, d, a_out, b_out, c_out, d_out, sems):
+    pairs = ((a, a_out), (b, b_out), (c, c_out), (d, d_out))
+    copies = [pltpu.make_async_copy(one, out, sems.at[i]) for i, (one, out) in enumerate(pairs)]
+    for copy in copies:
+        copy.start()
+    for copy in copies:
+        copy.wait()
 
 
 def on_device(layer_input, conv_output, state_maps, log_decay, out_grad):
@@ -578,16 +664,22 @@
         in_specs=[VMEM] * 5,
         out_specs=(VMEM,) * 4,
         scratch_shapes=[
-            floats(2, slices, ROWS, STATE),
-            floats(2, Z_SIZE, ROWS, STATE),
-            floats(2, Z_SIZE, ROWS, STATE),
-            floats(2, Z_SIZE, ROWS, STATE),
-            floats(2, Y_SIZE, ROWS, STATE),
-            floats(2, Z_SIZE, ROWS, STATE),
+            floats(2, slices, PAIR, STATE),
             floats(2, Z_SIZE, PAIR, STATE),
-            floats(2, Z_SIZE, PAIR, STATE),
-            floats(2, Z_SIZE, PAIR, STATE),
+            floats(CHUNKS, Z_SIZE, HEAD, STATE),
+            floats(CHUNKS, Z_SIZE, HEAD, STATE),
+            floats(CHUNKS, Y_SIZE, HEAD, STATE),
+            floats(CHUNKS, Z_SIZE, HEAD, STATE),
+            floats(CHUNKS, Z_SIZE, HEAD, STATE),
+            floats(CHUNKS, Z_SIZE, HEAD, STATE),
+            floats(CHUNKS, Z_SIZE, HEAD, STATE),
             floats(2, slices, PAIR, STATE),
+            floats(slices, 8, STATE),
+            floats(Z_SIZE, 8, STATE),
+            floats(Z_SIZE, 8, STATE),
+            floats(Z_SIZE, 8, STATE),
+            floats(Y_SIZE, 8, STATE),
+            floats(2, Z_SIZE, 8, STATE),
             floats(count, heads, 8, BLOCK),
             floats(count, heads, 8, STATE),
             floats(count, heads, BLOCK),
@@ -618,9 +710,10 @@
             floats(Y_SIZE, 2, z_rows, STATE),
             floats(2, 2, tile, STATE),
             floats(2, tile, STATE),
-            dma(2, Z_SIZE), dma(2, Z_SIZE), dma(2, Z_SIZE), dma(2, Z_SIZE),
-            dma(2, Y_SIZE), dma(2, Y_SIZE), dma(2, Z_SIZE), dma(2, Z_SIZE),
-            dma(2, Z_SIZE), dma(2, Z_SIZE),
+            dma(CHUNKS, Z_SIZE), dma(CHUNKS, Z_SIZE), dma(CHUNKS, Z_SIZE), dma(CHUNKS, Z_SIZE),
+            dma(CHUNKS, Y_SIZE), dma(CHUNKS, Y_SIZE), dma(CHUNKS, Z_SIZE), dma(CHUNKS, Z_SIZE),
+            dma(CHUNKS, Z_SIZE), dma(CHUNKS, Z_SIZE),
+            dma(1), dma(1), dma(Z_SIZE), dma(Z_SIZE), dma(Y_SIZE), dma(Y_SIZE),
             dma(2, 4), dma(2, 4), dma(2, 4), dma(2, 4),
             dma(2, Y_SIZE), dma(2, Y_SIZE), dma(Z_SIZE), dma(Z_SIZE),
             dma(2, Z_SIZE), dma(2, Z_SIZE), dma(Y_SIZE), dma(Y_SIZE),
@@ -631,7 +724,15 @@
         ),
         name="backward",
     )(conv_output, out_grad, state_maps, log_decay, layer_input)
-    return (grad_conv, grad_maps, grad_decay, grad_weight)
+    results = (grad_conv, grad_maps, grad_decay, grad_weight)
+    return pl.pallas_call(
+        hand_out_kernel,
+        out_shape=tuple(jax.ShapeDtypeStruct(one.shape, one.dtype) for one in results),
+        in_specs=[VMEM] * 4,
+        out_specs=(pl.BlockSpec(memory_space=pl.ANY),) * 4,
+        scratch_shapes=[dma(4)],
+        name="hand_out",
+    )(*results)
 
 
 def solution(mesh):

time: 128 us -> 114 us (0.89); the launches traced: 126 us -> 113 us
  Pallas kernels: 121 us -> 113 us
  local copies, waits for them, and re-layouts: 4.49 us -> 0 us
    pallas_call x1, Pallas kernels: 121 us -> 110 us  [on_device(): pl.pallas_call(functools.partial(kernel, 1.0 / math.sqrt(toks * lax.axis_...]
    unnamed x10 -> x0, local copies, waits for them, and re-layouts: 4.49 us -> none
    pallas_call x0 -> x1, Pallas kernels: none -> 2.41 us  [on_device(): pl.pallas_call(hand_out_kernel, out_shape=tuple((jax.ShapeDtypeStruct(one...]
where the time goes in v3:
time: 114 us; the launch traced here: 113 us
  Pallas kernels  113 us (99%)
    pallas_call x1, Pallas kernels, on_device(): pl.pallas_call(functools.partial(kernel, 1.0 / math.sqrt(toks * lax.axis_...  110 us
    pallas_call x1, Pallas kernels, on_device(): pl.pallas_call(hand_out_kernel, out_shape=tuple((jax.ShapeDtypeStruct(one...  2.41 us

profile of v3, /device:TPU:2, one launch (start us, length us, event | category | flops | bytes accessed | tf_op | source)
XLA Modules:
  0.0 113.3 jit_solution(11189932317020533617)
XLA Ops:
  0.6 110.2 %backward.1 = (bf16[256,2048]{1,0:T(8,128)(2,1)}, f32[256,256]{1,0:T(8,128)}, f32[32,256]{1,0:T(8,128)}, f32[32,256]{1,0:T(8,128)}) custom-call(bf16[256,2048]{1,0:T(8,128)(2,1)} %conv.1, bf16[256,2048]{1,0:T(8,128)(2,1)} %grad.1, bf16[256,256]{1,0:T(8,128)(2,1)} %maps.1, f32[32,256]{1,0:T(8,128)} %decay.1, bf16[256,2048]{1,0:T(8,128)(2,1)} %layer.1), custom_call_target="tpu_custom_call" | custom-call | tf_op jit(solution)/shard_map/backward/pallas_call | solution.py:656
  110.9 2.4 %hand_out.1 = (bf16[256,2048]{1,0:T(8,128)(2,1)}, f32[256,256]{1,0:T(8,128)}, f32[32,256]{1,0:T(8,128)}, f32[32,256]{1,0:T(8,128)}) custom-call(bf16[256,2048]{1,0:T(8,128)(2,1)} %get-tuple-element.8.a, f32[256,256]{1,0:T(8,128)} %get-tuple-element.9.b, f32[32,256]{1,0:T(8,128)} %get-tuple-element.10.c, f32[32,256]{1,0:T(8,128)} %get-tuple-element.11.d), custom_call_target="tpu_custom_call" | custom-call | tf_op jit(solution)/shard_map/hand_out/pallas_call | solution.py:728

commit v4 on v3

--- a/solution.py
+++ b/solution.py
@@ -73,17 +73,19 @@
 
 
 def kernel(
-    scale, z_rows,
+    scale, splits,
     conv, grad, maps, decay, layer, grad_conv, grad_maps, grad_decay, weight,
     own, x_in, t_out, z_in, y_in, before, back_out, back_in, x_out, result,
     d_own, d_x, d_t, d_z, d_y, d_before,
     cum_rows, total_rows, change, ends, mix, flow, wide, weighed, inner_out, finals, backs, states,
-    part, gathered, total, flipped, by_y0, by_y1, by_z,
-    ry_in0, ry_in1, rz_in, ry_sum0, ry_sum1, rz_sum, rz_late0, rz_late1, ry_late, rx_own, rx_in,
+    part, gathered, total, flipped, by_y, by_x, by_z,
+    ry_in, rx_in, rz_in, ry_sum, rx_sum, rz_sum, rz_late, ry_late, ry_next, ry_total, rz_next,
+    rl_own, rl_in,
     x_send, x_recv, z_send, z_recv, y_send, y_recv, b_send, b_recv, r_send, r_recv,
     dx_send, dx_recv, dz_send, dz_recv, dy_send, dy_recv,
     p_send, p_recv, g_send, g_recv, ry_send, ry_recv, rz_send, rz_recv,
-    rzl_send, rzl_recv, ryl_send, ryl_recv, rx_send, rx_recv,
+    rx_send, rx_recv, rzl_send, rzl_recv, ryl_send, ryl_recv, ryn_send, ryn_recv, rzn_send, rzn_recv,
+    rl_send, rl_recv,
 ):
     dp, y, z, x = place()
     other = device(dp, y, z, 1 - x)
@@ -321,12 +323,11 @@
             if k:
                 b_copy(chunk, k).start()
 
-    def hand_on(chunk, step):
+    def hand_on(chunk, k):
         way, part, rows = chunk // 2, chunk % 2, head_rows(chunk)
-        k = order(Z_SIZE - 1 - step)
         first = x == way
 
-        @pl.when(step > 0)
+        @pl.when(k > 0)
         def _():
             b_copy(chunk, k).wait_recv()
 
@@ -418,12 +419,17 @@
         return made.astype(BF16)
 
 
-    by_y, ry_in, ry_sum, rz_late = (by_y0, by_y1), (ry_in0, ry_in1), (ry_sum0, ry_sum1), (rz_late0, rz_late1)
-    splits = (0, z_rows)
-
     def ry_copy(half, m):
         return remote(
             by_y[half].at[(y + m) % Y_SIZE], ry_in[half].at[m], ry_send.at[half, m], ry_recv.at[half, m], y_at(m)
+        )
+
+    def rx_copy():
+        return remote(by_x.at[1 - x], rx_in, rx_send.at[0], rx_recv.at[0], other)
+
+    def rz_copy(half, k):
+        return remote(
+            by_z[half].at[(z + k) % Z_SIZE], rz_in[half].at[k], rz_send.at[half, k], rz_recv.at[half, k], z_at(k)
         )
 
     def rzl_copy(half, k):
@@ -432,64 +438,91 @@
             rzl_send.at[half, k], rzl_recv.at[half, k], z_at(k),
         )
 
-    def rz_copy(k):
-        return remote(by_z.at[(z + k) % Z_SIZE], rz_in.at[k], rz_send.at[k], rz_recv.at[k], z_at(k))
-
-    def ryl_copy(m):
-        return remote(
-            rz_sum.at[(y + m) % Y_SIZE], ry_late.at[m], ryl_send.at[m], ryl_recv.at[m], y_at(m)
-        )
-
-    def rx_copy(half):
-        return remote(
-            rx_own.at[half, 1 - x], rx_in.at[half], rx_send.at[half], rx_recv.at[half], other
+    def ryl_copy(half, m):
+        return remote(
+            rz_sum[half].at[(y + m) % Y_SIZE], ry_late[half].at[m],
+            ryl_send.at[half, m], ryl_recv.at[half, m], y_at(m),
+        )
+
+    def ryn_copy(m):
+        return remote(
+            rx_sum.at[(y + m) % Y_SIZE], ry_next.at[m], ryn_send.at[m], ryn_recv.at[m], y_at(m)
+        )
+
+    def rzn_copy(k):
+        return remote(
+            ry_total.at[(z + k) % Z_SIZE], rz_next.at[k], rzn_send.at[k], rzn_recv.at[k], z_at(k)
+        )
+
+    def rl_copy(half):
+        return remote(
+            rl_own[half].at[1 - x], rl_in[half], rl_send.at[half], rl_recv.at[half], other
         )
 
     def weigh(half, low):
-        cut = splits[half]
+        first, second, third = splits[half]
         for piece in range(Y_SIZE):
             made = dot(flipped[piece], low) * scale
             made = made.reshape(Z_SIZE, 2, -1, STATE)
-            by_y[half][piece] = made[:, :, cut:]
-            if cut:
-                by_z[:, piece] = made[:, :, :cut]
-        if cut:
-            for step in range(3):
-                rz_copy(order(step)).start()
+            by_z[half][:, piece] = made[:, :, :first]
+            by_y[half][piece] = made[:, :, first : first + second]
+            for side in range(2 if third else 0):
+                by_x[side, piece] = made[:, side, first + second :]
+        for step in range(3):
+            rz_copy(half, order(step)).start()
         for m in (2, 1, 3):
             ry_copy(half, m).start()
-        if cut:
-            for step in range(3, Z_SIZE - 1):
-                rz_copy(order(step)).start()
-
-    def weigh_middle(half):
+        if third:
+            rx_copy().start()
+        for step in range(3, Z_SIZE - 1):
+            rz_copy(half, order(step)).start()
+
+    def weigh_middle_x():
+        rx_copy().wait_recv()
+        rx_sum[...] = by_x[x] + rx_in[...]
+        for m in (2, 1, 3):
+            ryn_copy(m).start()
+
+    def weigh_middle_y(half):
         for m in range(1, Y_SIZE):
             ry_copy(half, m).wait_recv()
         ry_sum[half][...] = by_y[half][y] + ry_in[half][1] + ry_in[half][2] + ry_in[half][3]
         for step in range(Z_SIZE - 1):
             rzl_copy(half, order(step)).start()
 
-    def weigh_middle_z():
+    def weigh_middle_z(half):
         for k in range(1, Z_SIZE):
-            rz_copy(k).wait_recv()
-        rz_sum[...] = by_z[z] + sum(rz_in[k] for k in range(1, Z_SIZE))
+            rz_copy(half, k).wait_recv()
+        rz_sum[half][...] = by_z[half][z] + sum(rz_in[half][k] for k in range(1, Z_SIZE))
         for m in (2, 1, 3):
-            ryl_copy(m).start()
+            ryl_copy(half, m).start()
+
+    def weigh_next():
+        for m in range(1, Y_SIZE):
+            ryn_copy(m).wait_recv()
+        ry_total[...] = rx_sum[y] + sum(ry_next[m] for m in range(1, Y_SIZE))
+        for step in range(Z_SIZE - 1):
+            rzn_copy(order(step)).start()
 
     def weigh_late(half):
-        cut = splits[half]
-        if cut:
-            for m in range(1, Y_SIZE):
-                ryl_copy(m).wait_recv()
-            rx_own[half, :, :cut] = rz_sum[y] + sum(ry_late[m] for m in range(1, Y_SIZE))
+        first = splits[half][0]
+        for m in range(1, Y_SIZE):
+            ryl_copy(half, m).wait_recv()
+        rl_own[half][:, :first] = rz_sum[half][y] + sum(ry_late[half][m] for m in range(1, Y_SIZE))
         for k in range(1, Z_SIZE):
             rzl_copy(half, k).wait_recv()
-        rx_own[half, :, cut:] = ry_sum[half][z] + sum(rz_late[half][k] for k in range(1, Z_SIZE))
-        rx_copy(half).start()
+        rl_own[half][:, first:] = ry_sum[half][z] + sum(rz_late[half][k] for k in range(1, Z_SIZE))
+        rl_copy(half).start()
 
     def weigh_end(half):
-        rx_copy(half).wait_recv()
-        weight[:, (1 - half) * STATE : (2 - half) * STATE] = rx_own[half, x] + rx_in[half]
+        first, second, third = splits[half]
+        columns = slice((1 - half) * STATE, (2 - half) * STATE)
+        if third:
+            for k in range(1, Z_SIZE):
+                rzn_copy(k).wait_recv()
+            weight[first + second :, columns] = ry_total[z] + sum(rz_next[k] for k in range(1, Z_SIZE))
+        rl_copy(half).wait_recv()
+        weight[: first + second, columns] = rl_own[half][x] + rl_in[half][...]
 
 
     def done(turn):
@@ -531,75 +564,88 @@
     def nearest(step):
         return order(Z_SIZE - 1 - step)
 
-    def piece_of(half, step):
-        return half * Z_SIZE + (z + Z_SIZE - nearest(step)) % Z_SIZE
+    def own_then_far(step):
+        return order((step + Z_SIZE - 1) % Z_SIZE)
+
+    def piece_of(half, k):
+        return half * Z_SIZE + (z + Z_SIZE - k) % Z_SIZE
 
     def first_chunk(step, _):
-        hand_on(0, step)
+        hand_on(0, nearest(step))
         return 0
 
     def second_chunk(step, _):
-        hand_on(1, step)
-        with_start(piece_of(x, step))
-
-        @pl.when(step == 3)
-        def _():
-            spread(3)
-
+        hand_on(1, nearest(step))
         return 0
 
+    def own_first(step, _):
+        with_start(piece_of(x, nearest(step)))
+        return 0
+
+    def others_first(step, _):
+        k = nearest(step)
+        r_copy(0, k).wait_recv()
+        r_copy(1, k).wait_recv()
+        with_start(piece_of(1 - x, k))
+        return 0
+
     def third_chunk(step, _):
-        hand_on(2, step)
-        r_copy(0, nearest(step)).wait_recv()
-        r_copy(1, nearest(step)).wait_recv()
-        with_start(piece_of(1 - x, step))
+        hand_on(2, nearest(step))
         return 0
 
     def last_chunk(step, _):
-        hand_on(3, step)
-        with_finish(piece_of(x, step))
-
-        @pl.when(step == 3)
-        def _():
-            sum_middle(0)
-
+        hand_on(3, own_then_far(step))
         return 0
 
+    def own_last(step, _):
+        with_finish(piece_of(x, own_then_far(step)))
+        return 0
+
     def others_last(step, _):
-        r_copy(2, nearest(step)).wait_recv()
-        r_copy(3, nearest(step)).wait_recv()
-        with_finish(piece_of(1 - x, step))
+        k = own_then_far(step)
+        r_copy(2, k).wait_recv()
+        r_copy(3, k).wait_recv()
+        with_finish(piece_of(1 - x, k))
         return 0
 
     pass_decays()
     lax.fori_loop(0, Z_SIZE, joins, 0)
     lax.fori_loop(0, Z_SIZE, first_chunk, 0)
+    lax.fori_loop(0, Z_SIZE, second_chunk, 0)
     span = layer.shape[1] // Y_SIZE
     for piece in range(Y_SIZE):
         flipped[piece] = layer[:, piece * span : (piece + 1) * span].T
     scan(3)
-    lax.fori_loop(0, Z_SIZE, second_chunk, 0)
+    lax.fori_loop(0, Z_SIZE, own_first, 0)
+    spread(3)
+    lax.fori_loop(0, Z_SIZE // 2, others_first, 0)
     lax.fori_loop(0, Z_SIZE, third_chunk, 0)
+    lax.fori_loop(Z_SIZE // 2, Z_SIZE, others_first, 0)
     sum_begin(0)
+    sum_middle(0)
     lax.fori_loop(0, Z_SIZE, last_chunk, 0)
     low = sum_end(0)
     weigh(0, low)
+    lax.fori_loop(0, Z_SIZE, own_last, 0)
     lax.fori_loop(0, Z_SIZE, others_last, 0)
     sum_begin(1)
+    weigh_middle_y(0)
+    weigh_middle_z(0)
     sum_middle(1)
     low = sum_end(1)
     weigh(1, low)
+    weigh_late(0)
     for block in range(count):
         end_term = jnp.sum(jnp.sum(ends[block], axis=1), axis=1, keepdims=True)
         at_last = iota((heads, BLOCK), 1) == BLOCK - 1
         changes = change[block] + jnp.where(at_last, end_term, 0.0)
         grad_decay[:, blocks[block]] = dot(changes, lower, NN, HIGHEST)
-    weigh_middle(0)
-    weigh_middle_z()
-    weigh_middle(1)
-    weigh_late(0)
+    weigh_middle_x()
+    weigh_end(0)
+    weigh_middle_y(1)
+    weigh_next()
+    weigh_middle_z(1)
     weigh_late(1)
-    weigh_end(0)
     weigh_end(1)
 
     dx_copy().wait_send()
@@ -614,18 +660,21 @@
             y_copy(chunk, m).wait_send()
     for k in range(1, Z_SIZE):
         dz_copy(k).wait_send()
-        rz_copy(k).wait_send()
+        rzn_copy(k).wait_send()
         for half in range(2):
+            rz_copy(half, k).wait_send()
             rzl_copy(half, k).wait_send()
     for m in range(1, 4):
         dy_copy(m).wait_send()
-        ryl_copy(m).wait_send()
+        ryn_copy(m).wait_send()
         for half in range(2):
             p_copy(half, m).wait_send()
             g_copy(half, m).wait_send()
             ry_copy(half, m).wait_send()
+            ryl_copy(half, m).wait_send()
+    rx_copy().wait_send()
     for half in range(2):
-        rx_copy(half).wait_send()
+        rl_copy(half).wait_send()
 
 
 def dma(*shape):
@@ -647,14 +696,17 @@
     slices = heads // 2
     count = toks // BLOCK
     tile = columns // (Y_SIZE * Z_SIZE * 2)
-    z_rows = 8
-    late = tile - z_rows
+    splits = ((tile // 4, tile // 4 * 3, 0), (tile // 4, tile // 2, tile // 4))
+    third = splits[1][2]
 
     def floats(*shape):
         return pltpu.VMEM(shape, F32)
 
+    def both(which, *shape):
+        return [floats(*shape, splits[half][which], STATE) for half in range(2)]
+
     grad_conv, grad_maps, grad_decay, grad_weight = pl.pallas_call(
-        functools.partial(kernel, 1.0 / math.sqrt(toks * lax.axis_size("ctx")), z_rows),
+        functools.partial(kernel, 1.0 / math.sqrt(toks * lax.axis_size("ctx")), splits),
         out_shape=(
             jax.ShapeDtypeStruct((toks, columns), BF16),
             jax.ShapeDtypeStruct((toks, 2 * STATE), F32),
@@ -696,27 +748,30 @@
             floats(2, 4, toks // 4, STATE),
             floats(2, toks, STATE),
             pltpu.VMEM((Y_SIZE, columns // Y_SIZE, toks), BF16),
-            floats(Y_SIZE, Z_SIZE, 2, tile, STATE),
-            floats(Y_SIZE, Z_SIZE, 2, late, STATE),
-            floats(Z_SIZE, Y_SIZE, 2, z_rows, STATE),
-            floats(Y_SIZE, Z_SIZE, 2, tile, STATE),
-            floats(Y_SIZE, Z_SIZE, 2, late, STATE),
-            floats(Z_SIZE, Y_SIZE, 2, z_rows, STATE),
-            floats(Z_SIZE, 2, tile, STATE),
-            floats(Z_SIZE, 2, late, STATE),
-            floats(Y_SIZE, 2, z_rows, STATE),
-            floats(Z_SIZE, 2, tile, STATE),
-            floats(Z_SIZE, 2, late, STATE),
-            floats(Y_SIZE, 2, z_rows, STATE),
-            floats(2, 2, tile, STATE),
-            floats(2, tile, STATE),
+            both(1, Y_SIZE, Z_SIZE, 2),
+            floats(2, Y_SIZE, Z_SIZE, third, STATE),
+            both(0, Z_SIZE, Y_SIZE, 2),
+            both(1, Y_SIZE, Z_SIZE, 2),
+            floats(Y_SIZE, Z_SIZE, third, STATE),
+            both(0, Z_SIZE, Y_SIZE, 2),
+            both(1, Z_SIZE, 2),
+            floats(Y_SIZE, Z_SIZE, third, STATE),
+            both(0, Y_SIZE, 2),
+            both(1, Z_SIZE, 2),
+            both(0, Y_SIZE, 2),
+            floats(Y_SIZE, Z_SIZE, third, STATE),
+            floats(Z_SIZE, third, STATE),
+            floats(Z_SIZE, third, STATE),
+            [floats(2, sum(split[:2]), STATE) for split in splits],
+            [floats(sum(split[:2]), STATE) for split in splits],
             dma(CHUNKS, Z_SIZE), dma(CHUNKS, Z_SIZE), dma(CHUNKS, Z_SIZE), dma(CHUNKS, Z_SIZE),
             dma(CHUNKS, Y_SIZE), dma(CHUNKS, Y_SIZE), dma(CHUNKS, Z_SIZE), dma(CHUNKS, Z_SIZE),
             dma(CHUNKS, Z_SIZE), dma(CHUNKS, Z_SIZE),
             dma(1), dma(1), dma(Z_SIZE), dma(Z_SIZE), dma(Y_SIZE), dma(Y_SIZE),
             dma(2, 4), dma(2, 4), dma(2, 4), dma(2, 4),
-            dma(2, Y_SIZE), dma(2, Y_SIZE), dma(Z_SIZE), dma(Z_SIZE),
-            dma(2, Z_SIZE), dma(2, Z_SIZE), dma(Y_SIZE), dma(Y_SIZE),
+            dma(2, Y_SIZE), dma(2, Y_SIZE), dma(2, Z_SIZE), dma(2, Z_SIZE),
+            dma(1), dma(1), dma(2, Z_SIZE), dma(2, Z_SIZE), dma(2, Y_SIZE), dma(2, Y_SIZE),
+            dma(Y_SIZE), dma(Y_SIZE), dma(Z_SIZE), dma(Z_SIZE),
             dma(2), dma(2),
         ],
         compiler_params=pltpu.CompilerParams(

time: 114 us -> 111 us (0.974)
  Pallas kernels: 113 us -> 109 us
    pallas_call x1, Pallas kernels: 110 us -> 107 us  [on_device(): pl.pallas_call(functools.partial(kernel, 1.0 / math.sqrt(toks * lax.axis_...]
where the time goes in v4:
time: 111 us; the launch traced here: 110 us
  Pallas kernels  109 us (98%)
    pallas_call x1, Pallas kernels, on_device(): pl.pallas_call(functools.partial(kernel, 1.0 / math.sqrt(toks * lax.axis_...  107 us
    pallas_call x1, Pallas kernels, on_device(): pl.pallas_call(hand_out_kernel, out_shape=tuple((jax.ShapeDtypeStruct(one...  2.41 us

profile of v4, /device:TPU:2, one launch (start us, length us, event | category | flops | bytes accessed | tf_op | source)
XLA Modules:
  0.0 110.1 jit_solution(11204701722446616309)
XLA Ops:
  0.6 107.1 %backward.1 = (bf16[256,2048]{1,0:T(8,128)(2,1)}, f32[256,256]{1,0:T(8,128)}, f32[32,256]{1,0:T(8,128)}, f32[32,256]{1,0:T(8,128)}) custom-call(bf16[256,2048]{1,0:T(8,128)(2,1)} %conv.1, bf16[256,2048]{1,0:T(8,128)(2,1)} %grad.1, bf16[256,256]{1,0:T(8,128)(2,1)} %maps.1, f32[32,256]{1,0:T(8,128)} %decay.1, bf16[256,2048]{1,0:T(8,128)(2,1)} %layer.1), custom_call_target="tpu_custom_call" | custom-call | tf_op jit(solution)/shard_map/backward/pallas_call | solution.py:708
  107.7 2.4 %hand_out.1 = (bf16[256,2048]{1,0:T(8,128)(2,1)}, f32[256,256]{1,0:T(8,128)}, f32[32,256]{1,0:T(8,128)}, f32[32,256]{1,0:T(8,128)}) custom-call(bf16[256,2048]{1,0:T(8,128)(2,1)} %get-tuple-element.8.a, f32[256,256]{1,0:T(8,128)} %get-tuple-element.9.b, f32[32,256]{1,0:T(8,128)} %get-tuple-element.10.c, f32[32,256]{1,0:T(8,128)} %get-tuple-element.11.d), custom_call_target="tpu_custom_call" | custom-call | tf_op jit(solution)/shard_map/hand_out/pallas_call | solution.py:783

commit v5 on v4

--- a/solution.py
+++ b/solution.py
@@ -23,7 +23,7 @@
 TN = (((0,), (0,)), ((), ()))
 NN = (((1,), (0,)), ((), ()))
 VMEM = pl.BlockSpec(memory_space=pltpu.VMEM)
-LIMIT = 56 * 1024 * 1024
+LIMIT = 48 * 1024 * 1024
 
 
 def dot(a, b, dims=NN, precision=None):
@@ -78,7 +78,7 @@
     own, x_in, t_out, z_in, y_in, before, back_out, back_in, x_out, result,
     d_own, d_x, d_t, d_z, d_y, d_before,
     cum_rows, total_rows, change, ends, mix, flow, wide, weighed, inner_out, finals, backs, states,
-    part, gathered, total, flipped, by_y, by_x, by_z,
+    part, beside, total, across, flipped, by_y, by_x, by_z,
     ry_in, rx_in, rz_in, ry_sum, rx_sum, rz_sum, rz_late, ry_late, ry_next, ry_total, rz_next,
     rl_own, rl_in,
     x_send, x_recv, z_send, z_recv, y_send, y_recv, b_send, b_recv, r_send, r_recv,
@@ -379,42 +379,43 @@
                 state = fade_rows(block, index, state) + backs[block - 1, index]
 
 
-    share = toks // 4
-    mine = pl.ds(pl.multiple_of(dp * share, share), share)
-
-    def p_copy(half, m):
-        rows = pl.ds(pl.multiple_of((dp + m) % 4 * share, share), share)
-        return remote(
-            part.at[half, rows], gathered.at[half, m], p_send.at[half, m], p_recv.at[half, m], p_at(m)
-        )
-
-    def g_copy(half, m):
-        return remote(
-            total.at[half, mine], total.at[half, mine], g_send.at[half, m], g_recv.at[half, m], p_at(m)
-        )
+    core, chip = dp % 2, dp // 2
+    share = toks // 2
+
+    def p_copy(half):
+        return remote(
+            part.at[half], beside.at[half], p_send.at[half], p_recv.at[half],
+            device(dp + 1 - 2 * core, y, z, x),
+        )
+
+    def g_copy(half, source, target):
+        rows = pl.ds(pl.multiple_of(source * share, share), share)
+        return remote(
+            total.at[half, rows], across.at[half, rows], g_send.at[half, target], g_recv.at[half, source],
+            device((1 - chip) * 2 + target, y, z, x),
+        )
+
+    def mix_maps():
+        for block in range(count):
+            rows = blocks[block]
+            part[0, rows] = dot(mix[block], maps[rows, :STATE].astype(F32), NN, HIGHEST)
+            part[1, rows] = dot(mix[block], maps[rows, STATE:].astype(F32), TN, HIGHEST)
 
     def sum_begin(half):
         for block in range(count):
-            rows = blocks[block]
-            if half:
-                made = dot(mix[block], maps[rows, STATE:].astype(F32), TN, HIGHEST)
-            else:
-                made = dot(mix[block], maps[rows, :STATE].astype(F32), NN, HIGHEST)
-            part[half, rows] = made + flow[half, block]
-        for m in range(1, 4):
-            p_copy(half, m).start()
+            part[half, blocks[block]] += flow[half, block]
+        p_copy(half).start()
 
     def sum_middle(half):
-        for m in range(1, 4):
-            p_copy(half, m).wait_recv()
-        total[half, mine] = part[half, mine] + gathered[half, 1] + gathered[half, 2] + gathered[half, 3]
-        for m in range(1, 4):
-            g_copy(half, m).start()
+        p_copy(half).wait_recv()
+        total[half] = part[half] + beside[half]
+        for target in range(2):
+            g_copy(half, core, target).start()
 
     def sum_end(half):
-        for m in range(1, 4):
-            g_copy(half, m).wait_recv()
-        made = total[half]
+        for source in range(2):
+            g_copy(half, source, 0).wait_recv()
+        made = total[half] + across[half]
         grad_maps[:, (1 - half) * STATE : (2 - half) * STATE] = made
         return made.astype(BF16)
 
@@ -615,6 +616,7 @@
     span = layer.shape[1] // Y_SIZE
     for piece in range(Y_SIZE):
         flipped[piece] = layer[:, piece * span : (piece + 1) * span].T
+    mix_maps()
     scan(3)
     lax.fori_loop(0, Z_SIZE, own_first, 0)
     spread(3)
@@ -668,13 +670,14 @@
         dy_copy(m).wait_send()
         ryn_copy(m).wait_send()
         for half in range(2):
-            p_copy(half, m).wait_send()
-            g_copy(half, m).wait_send()
             ry_copy(half, m).wait_send()
             ryl_copy(half, m).wait_send()
     rx_copy().wait_send()
     for half in range(2):
         rl_copy(half).wait_send()
+        p_copy(half).wait_send()
+        for target in range(2):
+            g_copy(half, core, target).wait_send()
 
 
 def dma(*shape):
@@ -708,10 +711,10 @@
     grad_conv, grad_maps, grad_decay, grad_weight = pl.pallas_call(
         functools.partial(kernel, 1.0 / math.sqrt(toks * lax.axis_size("ctx")), splits),
         out_shape=(
-            jax.ShapeDtypeStruct((toks, columns), BF16),
-            jax.ShapeDtypeStruct((toks, 2 * STATE), F32),
-            jax.ShapeDtypeStruct((heads, toks), F32),
-            jax.ShapeDtypeStruct((tile, 2 * STATE), F32),
+            pltpu.VMEM((toks, columns), BF16),
+            pltpu.VMEM((toks, 2 * STATE), F32),
+            pltpu.VMEM((heads, toks), F32),
+            pltpu.VMEM((tile, 2 * STATE), F32),
         ),
         in_specs=[VMEM] * 5,
         out_specs=(VMEM,) * 4,
@@ -745,7 +748,8 @@
             floats(max(count - 1, 1), slices, PAIR, STATE),
             floats(count, slices, PAIR, STATE),
             floats(2, toks, STATE),
-            floats(2, 4, toks // 4, STATE),
+            floats(2, toks, STATE),
+            floats(2, toks, STATE),
             floats(2, toks, STATE),
             pltpu.VMEM((Y_SIZE, columns // Y_SIZE, toks), BF16),
             both(1, Y_SIZE, Z_SIZE, 2),
@@ -768,7 +772,7 @@
             dma(CHUNKS, Y_SIZE), dma(CHUNKS, Y_SIZE), dma(CHUNKS, Z_SIZE), dma(CHUNKS, Z_SIZE),
             dma(CHUNKS, Z_SIZE), dma(CHUNKS, Z_SIZE),
             dma(1), dma(1), dma(Z_SIZE), dma(Z_SIZE), dma(Y_SIZE), dma(Y_SIZE),
-            dma(2, 4), dma(2, 4), dma(2, 4), dma(2, 4),
+            dma(2), dma(2), dma(2, 2), dma(2, 2),
             dma(2, Y_SIZE), dma(2, Y_SIZE), dma(2, Z_SIZE), dma(2, Z_SIZE),
             dma(1), dma(1), dma(2, Z_SIZE), dma(2, Z_SIZE), dma(2, Y_SIZE), dma(2, Y_SIZE),
             dma(Y_SIZE), dma(Y_SIZE), dma(Z_SIZE), dma(Z_SIZE),
@@ -778,12 +782,20 @@
             collective_id=0, has_side_effects=True, vmem_limit_bytes=LIMIT
         ),
         name="backward",
-    )(conv_output, out_grad, state_maps, log_decay, layer_input)
-    results = (grad_conv, grad_maps, grad_decay, grad_weight)
+    )(
+        *(
+            pltpu.with_memory_space_constraint(one, pltpu.HBM)
+            for one in (conv_output, out_grad, state_maps, log_decay, layer_input)
+        )
+    )
+    results = [
+        pltpu.with_memory_space_constraint(one, pltpu.VMEM)
+        for one in (grad_conv, grad_maps, grad_decay, grad_weight)
+    ]
     return pl.pallas_call(
         hand_out_kernel,
         out_shape=tuple(jax.ShapeDtypeStruct(one.shape, one.dtype) for one in results),
-        in_specs=[VMEM] * 4,
+        in_specs=[pl.BlockSpec(memory_space=pl.ANY)] * 4,
         out_specs=(pl.BlockSpec(memory_space=pl.ANY),) * 4,
         scratch_shapes=[dma(4)],
         name="hand_out",

time: 111 us -> 108 us (0.973)
  Pallas kernels: 109 us -> 107 us
    pallas_call x1, Pallas kernels: 107 us -> 106 us  [on_device(): pl.pallas_call(functools.partial(kernel, 1.0 / math.sqrt(toks * lax.axis_...]
    pallas_call x1, Pallas kernels: 2.41 us -> 1.09 us  [on_device(): pl.pallas_call(hand_out_kernel, out_shape=tuple((jax.ShapeDtypeStruct(one...]
where the time goes in v5:
time: 108 us; the launch traced here: 107 us
  Pallas kernels  107 us (99%)
    pallas_call x1, Pallas kernels, on_device(): pl.pallas_call(functools.partial(kernel, 1.0 / math.sqrt(toks * lax.axis_...  106 us

profile of v5, /device:TPU:2, one launch (start us, length us, event | category | flops | bytes accessed | tf_op | source)
XLA Modules:
  0.0 107.4 jit_solution(1780939619467526384)
XLA Ops:
  0.6 105.7 %backward.1 = (bf16[256,2048]{1,0:T(8,128)(2,1)S(1)}, f32[256,256]{1,0:T(8,128)S(1)}, f32[32,256]{1,0:T(8,128)S(1)}, f32[32,256]{1,0:T(8,128)S(1)}) custom-call(bf16[256,2048]{1,0:T(8,128)(2,1)} %conv.1, bf16[256,2048]{1,0:T(8,128)(2,1)} %grad.1, bf16[256,256]{1,0:T(8,128)(2,1)} %maps.1, f32[32,256]{1,0:T(8,128)} %decay.1, bf16[256,2048]{1,0:T(8,128)(2,1)} %layer.1), custom_call_target="tpu_custom_call" | custom-call | tf_op jit(solution)/shard_map/backward/pallas_call | solution.py:711
  106.3 1.1 %hand_out.1 = (bf16[256,2048]{1,0:T(8,128)(2,1)}, f32[256,256]{1,0:T(8,128)}, f32[32,256]{1,0:T(8,128)}, f32[32,256]{1,0:T(8,128)}) custom-call(bf16[256,2048]{1,0:T(8,128)(2,1)S(1)} %get-tuple-element.8.a, f32[256,256]{1,0:T(8,128)S(1)} %get-tuple-element.9.b, f32[32,256]{1,0:T(8,128)S(1)} %get-tuple-element.10.c, f32[32,256]{1,0:T(8,128)S(1)} %get-tuple-element.11.d), custom_call_target="tpu_custom_call" | custom-call | tf_op jit(solution)/shard_map/hand_out/pallas_call | solution.py:795

commit v6 on v5

--- a/solution.py
+++ b/solution.py
@@ -631,23 +631,23 @@
     lax.fori_loop(0, Z_SIZE, own_last, 0)
     lax.fori_loop(0, Z_SIZE, others_last, 0)
     sum_begin(1)
+    sum_middle(1)
     weigh_middle_y(0)
     weigh_middle_z(0)
-    sum_middle(1)
     low = sum_end(1)
     weigh(1, low)
-    weigh_late(0)
     for block in range(count):
         end_term = jnp.sum(jnp.sum(ends[block], axis=1), axis=1, keepdims=True)
         at_last = iota((heads, BLOCK), 1) == BLOCK - 1
         changes = change[block] + jnp.where(at_last, end_term, 0.0)
         grad_decay[:, blocks[block]] = dot(changes, lower, NN, HIGHEST)
     weigh_middle_x()
-    weigh_end(0)
     weigh_middle_y(1)
     weigh_next()
     weigh_middle_z(1)
+    weigh_late(0)
     weigh_late(1)
+    weigh_end(0)
     weigh_end(1)
 
     dx_copy().wait_send()

time: 108 us -> 105 us (0.972)
  Pallas kernels: 107 us -> 104 us
    pallas_call x1, Pallas kernels: 106 us -> 102 us  [on_device(): pl.pallas_call(functools.partial(kernel, 1.0 / math.sqrt(toks * lax.axis_...]
where the time goes in v6:
time: 105 us; the launch traced here: 104 us
  Pallas kernels  104 us (99%)
    pallas_call x1, Pallas kernels, on_device(): pl.pallas_call(functools.partial(kernel, 1.0 / math.sqrt(toks * lax.axis_...  102 us

profile of v6, /device:TPU:2, one launch (start us, length us, event | category | flops | bytes accessed | tf_op | source)
XLA Modules:
  0.0 104.2 jit_solution(8044628618922374644)
XLA Ops:
  0.6 102.4 %backward.1 = (bf16[256,2048]{1,0:T(8,128)(2,1)S(1)}, f32[256,256]{1,0:T(8,128)S(1)}, f32[32,256]{1,0:T(8,128)S(1)}, f32[32,256]{1,0:T(8,128)S(1)}) custom-call(bf16[256,2048]{1,0:T(8,128)(2,1)} %conv.1, bf16[256,2048]{1,0:T(8,128)(2,1)} %grad.1, bf16[256,256]{1,0:T(8,128)(2,1)} %maps.1, f32[32,256]{1,0:T(8,128)} %decay.1, bf16[256,2048]{1,0:T(8,128)(2,1)} %layer.1), custom_call_target="tpu_custom_call" | custom-call | tf_op jit(solution)/shard_map/backward/pallas_call | solution.py:711
  103.1 1.1 %hand_out.1 = (bf16[256,2048]{1,0:T(8,128)(2,1)}, f32[256,256]{1,0:T(8,128)}, f32[32,256]{1,0:T(8,128)}, f32[32,256]{1,0:T(8,128)}) custom-call(bf16[256,2048]{1,0:T(8,128)(2,1)S(1)} %get-tuple-element.8.a, f32[256,256]{1,0:T(8,128)S(1)} %get-tuple-element.9.b, f32[32,256]{1,0:T(8,128)S(1)} %get-tuple-element.10.c, f32[32,256]{1,0:T(8,128)S(1)} %get-tuple-element.11.d), custom_call_target="tpu_custom_call" | custom-call | tf_op jit(solution)/shard_map/hand_out/pallas_call | solution.py:795

commit v7 on v6

--- a/solution.py
+++ b/solution.py
@@ -23,6 +23,7 @@
 TN = (((0,), (0,)), ((), ()))
 NN = (((1,), (0,)), ((), ()))
 VMEM = pl.BlockSpec(memory_space=pltpu.VMEM)
+FAR = pl.BlockSpec(memory_space=pl.ANY)
 LIMIT = 48 * 1024 * 1024
 
 
@@ -37,6 +38,11 @@
 def two_parts(values):
     high = values.astype(BF16)
     return high, (values - high.astype(F32)).astype(BF16)
+
+
+def three_parts(values):
+    high, rest = two_parts(values)
+    return high, rest, (values - high.astype(F32) - rest.astype(F32)).astype(BF16)
 
 
 def head_lanes(first_head, head_count, columns, width):
@@ -74,7 +80,7 @@
 
 def kernel(
     scale, splits,
-    conv, grad, maps, decay, layer, grad_conv, grad_maps, grad_decay, weight,
+    conv, grad_far, maps, decay, layer_far, grad_conv, grad_maps, grad_decay, weight,
     own, x_in, t_out, z_in, y_in, before, back_out, back_in, x_out, result,
     d_own, d_x, d_t, d_z, d_y, d_before,
     cum_rows, total_rows, change, ends, mix, flow, wide, weighed, inner_out, finals, backs, states,
@@ -85,8 +91,14 @@
     dx_send, dx_recv, dz_send, dz_recv, dy_send, dy_recv,
     p_send, p_recv, g_send, g_recv, ry_send, ry_recv, rz_send, rz_recv,
     rx_send, rx_recv, rzl_send, rzl_recv, ryl_send, ryl_recv, ryn_send, ryn_recv, rzn_send, rzn_recv,
-    rl_send, rl_recv,
+    rl_send, rl_recv, grad, layer, load_sems,
 ):
+    loads = [
+        pltpu.make_async_copy(far, near, load_sems.at[one])
+        for one, (far, near) in enumerate(((grad_far, grad), (layer_far, layer)))
+    ]
+    for load in loads:
+        load.start()
     dp, y, z, x = place()
     other = device(dp, y, z, 1 - x)
 
@@ -156,13 +168,14 @@
 
 
     decays = decay[...]
-    lower_all = (iota((toks, toks), 1) <= iota((toks, toks), 0)).astype(F32)
-    cum_all = dot(lower_all, decays, NT, HIGHEST)
+    lower_all = (iota((toks, toks), 1) <= iota((toks, toks), 0)).astype(BF16)
+    decay_parts = three_parts(decays)
+    cum_all = sum(dot(lower_all, piece, NT) for piece in decay_parts)
     factors = (two_parts(jnp.exp(cum_all[toks - 1 : toks, :] - cum_all)), two_parts(jnp.exp(cum_all)))
     sources = (conv, grad)
-    total_all = jnp.exp(dot(decays, jnp.ones((toks, STATE), F32), NN, HIGHEST))
-    expand = (iota((heads * 4, heads), 0) // 4 == iota((heads * 4, heads), 1)).astype(F32)
-    d_own[...] = dot(expand, total_all, NN, HIGHEST).reshape(heads // 2, 8, STATE)
+    total_all = jnp.exp(sum(dot(piece, jnp.ones((toks, STATE), BF16)) for piece in decay_parts))
+    expand = (iota((heads * 4, heads), 0) // 4 == iota((heads * 4, heads), 1)).astype(BF16)
+    d_own[...] = sum(dot(expand, piece) for piece in three_parts(total_all)).reshape(heads // 2, 8, STATE)
 
     def summarize(way, half):
         chunk = 8 * HEAD
@@ -180,6 +193,7 @@
     for chunk in range(2):
         for step in range(Z_SIZE):
             x_copy(chunk, order(step)).start()
+    loads[0].wait()
     summarize(1, 1 - x)
     for chunk in range(2, CHUNKS):
         for step in range(Z_SIZE):
@@ -462,17 +476,18 @@
 
     def weigh(half, low):
         first, second, third = splits[half]
-        for piece in range(Y_SIZE):
+        for m in (2, 1, 3, 0):
+            piece = (y + m) % Y_SIZE
             made = dot(flipped[piece], low) * scale
             made = made.reshape(Z_SIZE, 2, -1, STATE)
             by_z[half][:, piece] = made[:, :, :first]
             by_y[half][piece] = made[:, :, first : first + second]
             for side in range(2 if third else 0):
                 by_x[side, piece] = made[:, side, first + second :]
+            if m:
+                ry_copy(half, m).start()
         for step in range(3):
             rz_copy(half, order(step)).start()
-        for m in (2, 1, 3):
-            ry_copy(half, m).start()
         if third:
             rx_copy().start()
         for step in range(3, Z_SIZE - 1):
@@ -613,6 +628,7 @@
     lax.fori_loop(0, Z_SIZE, joins, 0)
     lax.fori_loop(0, Z_SIZE, first_chunk, 0)
     lax.fori_loop(0, Z_SIZE, second_chunk, 0)
+    loads[1].wait()
     span = layer.shape[1] // Y_SIZE
     for piece in range(Y_SIZE):
         flipped[piece] = layer[:, piece * span : (piece + 1) * span].T
@@ -716,7 +732,7 @@
             pltpu.VMEM((heads, toks), F32),
             pltpu.VMEM((tile, 2 * STATE), F32),
         ),
-        in_specs=[VMEM] * 5,
+        in_specs=[VMEM, FAR, VMEM, VMEM, FAR],
         out_specs=(VMEM,) * 4,
         scratch_shapes=[
             floats(2, slices, PAIR, STATE),
@@ -777,6 +793,7 @@
             dma(1), dma(1), dma(2, Z_SIZE), dma(2, Z_SIZE), dma(2, Y_SIZE), dma(2, Y_SIZE),
             dma(Y_SIZE), dma(Y_SIZE), dma(Z_SIZE), dma(Z_SIZE),
             dma(2), dma(2),
+            pltpu.VMEM((toks, columns), BF16), pltpu.VMEM((toks, columns), BF16), dma(2),
         ],
         compiler_params=pltpu.CompilerParams(
             collective_id=0, has_side_effects=True, vmem_limit_bytes=LIMIT

time: 105 us -> 105 us (level)
  no operation moved by 1% of the time
where the time goes in v7:
time: 105 us; the launch traced here: 104 us
  Pallas kernels  103 us (98%)
    pallas_call x1, Pallas kernels, on_device(): pl.pallas_call(functools.partial(kernel, 1.0 / math.sqrt(toks * lax.axis_...  102 us

profile of v7, /device:TPU:2, one launch (start us, length us, event | category | flops | bytes accessed | tf_op | source)
XLA Modules:
  0.0 103.8 jit_solution(2318132781468902204)
XLA Ops:
  0.6 102.1 %backward.1 = (bf16[256,2048]{1,0:T(8,128)(2,1)S(1)}, f32[256,256]{1,0:T(8,128)S(1)}, f32[32,256]{1,0:T(8,128)S(1)}, f32[32,256]{1,0:T(8,128)S(1)}) custom-call(bf16[256,2048]{1,0:T(8,128)(2,1)} %conv.1, bf16[256,2048]{1,0:T(8,128)(2,1)} %grad_far.1, bf16[256,256]{1,0:T(8,128)(2,1)} %maps.1, f32[32,256]{1,0:T(8,128)} %decay.1, bf16[256,2048]{1,0:T(8,128)(2,1)} %layer_far.1), custom_call_target="tpu_custom_call" | custom-call | tf_op jit(solution)/shard_map/backward/pallas_call | solution.py:727
  102.8 1.1 %hand_out.1 = (bf16[256,2048]{1,0:T(8,128)(2,1)}, f32[256,256]{1,0:T(8,128)}, f32[32,256]{1,0:T(8,128)}, f32[32,256]{1,0:T(8,128)}) custom-call(bf16[256,2048]{1,0:T(8,128)(2,1)S(1)} %get-tuple-element.8.a, f32[256,256]{1,0:T(8,128)S(1)} %get-tuple-element.9.b, f32[32,256]{1,0:T(8,128)S(1)} %get-tuple-element.10.c, f32[32,256]{1,0:T(8,128)S(1)} %get-tuple-element.11.d), custom_call_target="tpu_custom_call" | custom-call | tf_op jit(solution)/shard_map/hand_out/pallas_call | solution.py:812
